TPU v7x, 128 devices: a whole 4x4x4 slice. The times are simulated.
128 devices in a mesh: dp: 16 (over z_lo, x, core), tile: 8 (over z_hi, y).
Axes of the slice: x: 4, y: 4, z: 4 (z_hi: 2, z_lo: 2; z = z_hi * 2 + z_lo), core: 2. Of those that a mesh axis runs over, the one named last changes fastest.
Arguments:
- features: bfloat16 [16, 64, 128, 640], P('dp', 'tile'), may hold values from -48 to 48
- cotangent: bfloat16 [16, 64, 128, 640], P('dp', 'tile'), may hold values from -6 to 6
- mask: int32 [16, 64, 128], P('dp', 'tile'), may hold values 0 or 1
- conv_weight: bfloat16 [3, 3, 640, 640], replicated, may hold values from -0.078125 to 0.078125
- gamma: float32 [640], replicated, may hold values from 0.1 to 1.9
- beta: float32 [640], replicated, may hold values from -3 to 3
Outputs:
- dfeatures: bfloat16 [16, 64, 128, 640], P('dp', 'tile')
- dweight: float32 [5760, 640], P('tile')
- dgains: float32 [2, 640], replicated
All inputs are finite; a program needn't handle non-finite values. No bound on the sum of `mask` on one device may be relied on, other than what follows from the above.
Results may differ from a plain program's by a relative error of at most 0.0029.
Values may be sent and summed in bfloat16 or wider, within the bound.
A program may use at most 128 MiB of HBM per device.

v0:
```python
import jax
import jax.numpy as jnp
from jax import lax
from jax.sharding import PartitionSpec as P

G = 32


EPSILON = 1e-05


def with_halo(value, sides, width):
    for axis, dim in sides:
        size, length = (lax.axis_size(axis), value.shape[dim])
        up = [(i, (i + 1) % size) for i in range(size - 1)]
        down = [(j, i) for i, j in up]
        last = lax.slice_in_dim(value, length - width, length, axis=dim)
        leading = lax.slice_in_dim(value, 0, width, axis=dim)
        before = lax.ppermute(last, axis, up)
        after = lax.ppermute(leading, axis, down)
        value = jnp.concatenate([before, value, after], axis=dim)
    return value


def unfold(padded, row_count, col_count):
    pieces = [
        padded[offset_y : offset_y + row_count, offset_x : offset_x + col_count, :]
        for offset_y in range(3)
        for offset_x in range(3)
    ]
    joined = jnp.concatenate(pieces, axis=-1)
    return joined.reshape(row_count * col_count, joined.shape[-1])


def unfold_channels(padded, row_count, col_count):
    pieces = [
        padded[offset_y : offset_y + row_count, offset_x : offset_x + col_count, :]
        for offset_y in range(3)
        for offset_x in range(3)
    ]
    joined = jnp.stack(pieces, axis=-1)
    return joined.reshape(row_count * col_count, joined.shape[-2] * 9)


def shards(features, cotangent, mask, conv_weight, gamma, beta):
    row_count, col_count, channels = (features.shape[1], features.shape[2], features.shape[3])
    per_group = channels // G
    strips = lax.axis_size("tile")
    cell_count = float(row_count * strips * col_count * per_group)
    grouped = features[0].astype(jnp.float32).reshape(row_count, col_count, G, per_group)
    group_total = lax.psum(jnp.sum(grouped, axis=(0, 1, 3)), "tile")
    group_mean = group_total / cell_count
    centered = grouped - group_mean[None, None, :, None]
    variance = lax.psum(jnp.sum(centered * centered, axis=(0, 1, 3)), "tile") / cell_count
    inverse = lax.rsqrt(variance + EPSILON)
    scaled_groups = centered * inverse[None, None, :, None]
    scaled = scaled_groups.reshape(row_count, col_count, channels)
    normed = scaled * gamma + beta
    active = jax.nn.silu(normed).astype(jnp.bfloat16)
    weighted = (
        cotangent[0].astype(jnp.float32) * (1.0 + mask[0].astype(jnp.float32))[:, :, None]
    ).astype(jnp.bfloat16)
    grad_rows = weighted.reshape(row_count * col_count, channels)
    act_rows = with_halo(active, (("tile", 0),), 1)
    act_cols = unfold_channels(jnp.pad(act_rows, ((0, 0), (1, 1), (0, 0))), row_count, col_count)
    local_grad = lax.psum_scatter(
        lax.dot_general(
            act_cols, grad_rows, (((0,), (0,)), ((), ())), preferred_element_type=jnp.float32
        ),
        "tile",
        scatter_dimension=0,
        tiled=True,
    )
    dweight = lax.psum(local_grad, "dp")
    flipped_mat = conv_weight[::-1, ::-1].transpose(0, 1, 3, 2).reshape(9 * channels, channels)
    grad_padded = with_halo(weighted, (("tile", 0),), 1)
    grad_cols = unfold(jnp.pad(grad_padded, ((0, 0), (1, 1), (0, 0))), row_count, col_count)
    dactive = jnp.dot(grad_cols, flipped_mat, preferred_element_type=jnp.float32).reshape(
        row_count, col_count, channels
    )
    sigmoid_val = jax.nn.sigmoid(normed)
    dnormed = dactive * sigmoid_val * (1.0 + normed * (1.0 - sigmoid_val))
    local_gains = jnp.stack([jnp.sum(dnormed * scaled, axis=(0, 1)), jnp.sum(dnormed, axis=(0, 1))])
    dgains = lax.psum(local_gains, ("dp", "tile"))
    dscaled = (dnormed * gamma).reshape(row_count, col_count, G, per_group)
    first_sum, second_sum = lax.psum(
        (jnp.sum(dscaled, axis=(0, 1, 3)), jnp.sum(dscaled * scaled_groups, axis=(0, 1, 3))), "tile"
    )
    first_moment = first_sum / cell_count
    second_moment = second_sum / cell_count
    dinput = inverse[None, None, :, None] * (
        dscaled
        - first_moment[None, None, :, None]
        - scaled_groups * second_moment[None, None, :, None]
    )
    dinput = dinput.reshape(row_count, col_count, channels) + weighted.astype(jnp.float32)
    return (dinput.astype(jnp.bfloat16)[None], dweight, dgains)


def solution(mesh):
    placed = (
        P("dp", "tile", None, None),
        P("dp", "tile", None, None),
        P("dp", "tile", None),
        P(),
        P(),
        P(),
    )
    return jax.shard_map(
        shards,
        mesh=mesh,
        in_specs=placed,
        out_specs=(P("dp", "tile", None, None), P("tile", None), P()),
        check_vma=False,
    )
```

profile of v0, /device:TPU:1, one launch (start us, length us, event | category | flops | bytes accessed | tf_op | source)
XLA Modules:
  0.0 482.5 jit_solution(2540591238833873730)
XLA Ops:
  7.2 0.8 add_bitcast_fusion
  8.0 1.6 fusion.5
  9.7 4.0 collective-permute-start
  13.7 1.3 collective-permute-start.1
  15.0 0.2 convert_reduce_fusion
  15.4 0.1 reduce_sum.67
  15.5 22.3 %psum.42 = f32[32]{0:T(128)S(1)} all-reduce(f32[32]{0:T(128)S(1)} %reduce_sum.67), channel_id=1, replica_groups=mesh['dp'=16,'tile'=8] {'tile'}, use_global_device_ids=true, to_apply=%region_2.0 | all-reduce | flops 32 | bytes 256 | tf_op jit(solution)/shard_map/psum | solution.py:51
  38.0 0.4 fusion.8
  38.6 15.5 %psum.43 = f32[32]{0:T(128)S(1)} all-reduce(f32[32]{0:T(128)S(1)} %reduce_sum.73), channel_id=1, replica_groups=mesh['dp'=16,'tile'=8] {'tile'}, use_global_device_ids=true, to_apply=%region_5.6 | all-reduce | flops 32 | bytes 256 | tf_op jit(solution)/shard_map/psum | solution.py:54
  54.3 12.4 %copy.9 = bf16[3,3,640,640]{2,3,1,0:T(8,128)(2,1)} copy(bf16[3,3,640,640]{3,2,1,0:T(8,128)(2,1)} %param.9) | data formatting | bytes 14745600 | tf_op args[3]
  66.7 6.9 %rev.3 = bf16[3,3,640,640]{2,3,1,0:T(8,128)(2,1)} reverse(bf16[3,3,640,640]{2,3,1,0:T(8,128)(2,1)} %copy.9), dimensions={0,1} | reverse | bytes 14745600 | tf_op jit(solution)/shard_map/rev | solution.py:75
  73.7 0.4 select_maximum_fusion.2
  74.1 0.1 slice_dynamic-update-slice_fusion.5
  74.2 0.2 fusion.55
  74.5 0.4 slice_dynamic-update-slice_fusion.4
  74.9 0.2 slice_dynamic-update-slice_fusion.3
  75.2 0.6 copy-done
  75.8 0.4 constant_dynamic-update-slice_fusion
  76.2 0.4 slice_dynamic-update-slice_fusion.2
  76.6 0.2 slice_dynamic-update-slice_fusion.1
  76.9 0.2 fusion.54
  77.1 0.4 slice_dynamic-update-slice_fusion
  77.5 0.8 slice-done.1
  78.3 0.3 copy-done.2
  78.6 12.0 %fusion.30 = (f32[640]{0:T(1024)S(1)}, f32[640]{0:T(1024)S(1)}, f32[640]{0:T(1024)S(1)}, f32[640]{0:T(1024)S(1)}, f32[8,128,640]{2,1,0:T(8,128)}) fusion(bf16[1,8,128,640]{3,2,1,0:T(8,128)(2,1)S(1)} %copy-done.2, f32[640]{0:T(1024)S(1)} %sub.50, f32[640]{0:T(1024)S(1)} %mul.114, f32[640]{0:T(1024)S(1)} %copy-done.6, f32[640]{0:T(1024)S(1)} %copy-done.5, ...), kind=kOutput, calls=%fused_computation.38 | convolution fusion | flops 7562852352 | bytes 23121920 | tf_op jit(solution)/shard_map/dot_general | solution.py:78
  90.9 0.1 reduce_sum.93
  91.0 17.4 %all-reduce.2 = (f32[32]{0:T(128)S(1)}, f32[32]{0:T(128)S(1)}) all-reduce(f32[32]{0:T(128)S(1)} %reduce_sum.93, f32[32]{0:T(128)S(1)} %reduce_sum.90), channel_id=1, replica_groups=mesh['dp'=16,'tile'=8] {'tile'}, use_global_device_ids=true, to_apply=%region_11.12 | all-reduce | flops 64 | bytes 512 | tf_op jit(solution)/shard_map/psum | solution.py:86
  108.7 3.9 fusion.24
  112.6 1.7 collective-permute-start.2
  114.3 1.3 collective-permute-start.3
  115.6 1.3 fusion.6
  116.9 3.4 collective-permute-done.3
  120.3 0.5 select_maximum_fusion
  120.8 1.2 fusion.53
  122.0 1.2 fusion.52
  123.2 1.4 fusion.50
  124.6 1.2 fusion.49
  125.9 2.0 fusion.42
  127.9 1.4 fusion.48
  129.3 1.3 fusion.47
  130.6 1.2 fusion.46
  131.7 1.4 fusion.44
  133.1 16.2 %copy.10 = bf16[8,128,640,9]{1,0,3,2:T(8,128)(2,1)} copy(bf16[8,128,640,9]{2,1,0,3:T(8,128)(2,1)} %fusion.44) | data formatting | bytes 23592960 | tf_op jit(solution)/shard_map/stack | solution.py:41
  149.3 15.3 %fusion = f32[5760,640]{1,0:T(8,128)} fusion(bf16[1024,640]{1,0:T(8,128)(2,1)S(1)} %bitcast.144, bf16[720,8,8,128]{3,2,1,0:T(8,128)(2,1)} %bitcast.140), kind=kOutput, calls=%fused_computation | convolution fusion | flops 7549747200 | bytes 27852800 | tf_op jit(solution)/shard_map/dot_general | solution.py:67
  164.7 187.8 %reduce-scatter.2.cloned.1.call-done = f32[720,640]{1,0:T(8,128)} async-done(((f32[5760,640]{1,0:T(8,128)}), f32[720,640]{1,0:T(8,128)}) %reduce-scatter.2.cloned.1.call-update) | async-done | bytes 1843216 | tf_op jit(solution)/shard_map/reduce_scatter | solution.py:66
  352.5 64.8 %psum.47 = f32[2,640]{1,0:T(2,128)} all-reduce(f32[2,640]{1,0:T(2,128)S(1)} %pad_maximum_fusion.4), channel_id=1, replica_groups=mesh['dp'=16,'tile'=8] {'dp','tile'}, use_global_device_ids=true, to_apply=%region_16.17 | all-reduce | flops 1280 | bytes 10240 | tf_op jit(solution)/shard_map/psum | solution.py:84
  417.3 55.5 %all-reduce.5.cloned.1.call-done = f32[720,640]{1,0:T(8,128)} async-done(((f32[720,640]{1,0:T(8,128)}), f32[720,640]{1,0:T(8,128)}) %all-reduce.5.cloned.1.call-update) | async-done | bytes 1843216 | tf_op jit(solution)/shard_map/psum | solution.py:74
  472.8 2.9 copy.33
  (45 shorter events, 1.6 us)
Async XLA Ops:
  7.2 7.8 %copy-start.1 = (bf16[1,8,128,640]{3,2,1,0:T(8,128)(2,1)S(1)}, bf16[1,8,128,640]{3,2,1,0:T(8,128)(2,1)}, u32[]{:S(2)}) copy-start(bf16[1,8,128,640]{3,2,1,0:T(8,128)(2,1)} %param.6) | copy-start | bytes 3932164
  7.2 345.3 %reduce-scatter.2.cloned.1.call-start = ((), (), s32[]{:S(2)}) async-start(), calls=%async_computation.1 | async-start | bytes 16588800 | tf_op jit(solution)/shard_map/reduce_scatter | solution.py:66
  9.7 64.0 %collective-permute-start = (bf16[1,128,640]{2,1,0:T(8,128)(2,1)S(1)}, bf16[1,128,640]{2,1,0:T(8,128)(2,1)S(1)}, u32[]{:S(2)}, u32[]{:S(2)}) collective-permute-start(bf16[1,128,640]{2,1,0:T(8,128)(2,1)S(1)} %get-tuple-element.13), channel_id=1, source_target_pairs={{0,1},{1,2},{2,3},{3,4},{4,5},{5,6},{6,7},{8,9},{9,10},{10,11},{11... | collective-permute-start | bytes 491528 | tf_op jit(solution)/shard_map/ppermute | solution.py:19
  13.7 60.0 %collective-permute-start.1 = (bf16[1,128,640]{2,1,0:T(8,128)(2,1)S(1)}, bf16[1,128,640]{2,1,0:T(8,128)(2,1)S(1)}, u32[]{:S(2)}, u32[]{:S(2)}) collective-permute-start(bf16[1,128,640]{2,1,0:T(8,128)(2,1)S(1)} %get-tuple-element.14), channel_id=1, source_target_pairs={{1,0},{2,1},{3,2},{4,3},{5,4},{6,5},{7,6},{9,8},{10,9},{11,10},{12... | collective-permute-start | bytes 491528 | tf_op jit(solution)/shard_map/ppermute | solution.py:20
  74.5 1.3 copy-start
  74.5 3.0 slice-start
  76.2 2.1 slice-start.1
  76.8 1.7 copy-start.2
  76.9 1.7 copy-start.5
  76.9 1.7 copy-start.6
  78.6 30.2 %copy-start.3 = (bf16[1,8,128,640]{3,2,1,0:T(8,128)(2,1)S(1)}, bf16[1,8,128,640]{3,2,1,0:T(8,128)(2,1)}, u32[]{:S(2)}) copy-start(bf16[1,8,128,640]{3,2,1,0:T(8,128)(2,1)} %param.6) | copy-start | bytes 3932164
  112.6 4.3 collective-permute-start.2
  114.3 6.1 %collective-permute-start.3 = (bf16[1,128,640]{2,1,0:T(8,128)(2,1)S(1)}, bf16[1,128,640]{2,1,0:T(8,128)(2,1)S(1)}, u32[]{:S(2)}, u32[]{:S(2)}) collective-permute-start(bf16[1,128,640]{2,1,0:T(8,128)(2,1)S(1)} %get-tuple-element.12), channel_id=1, source_target_pairs={{1,0},{2,1},{3,2},{4,3},{5,4},{6,5},{7,6},{9,8},{10,9},{11,10},{12... | collective-permute-start | bytes 491528 | tf_op jit(solution)/shard_map/ppermute | solution.py:20
  133.1 16.2 %copy-start.4 = (bf16[1,8,128,640]{3,2,1,0:T(8,128)(2,1)S(1)}, bf16[1,8,128,640]{3,2,1,0:T(8,128)(2,1)}, u32[]{:S(2)}) copy-start(bf16[1,8,128,640]{3,2,1,0:T(8,128)(2,1)} %fusion.6) | copy-start | bytes 3932164
  164.6 308.2 %all-reduce.5.cloned.1.call-start = ((), (), s32[]{:S(2)}) async-start(), calls=%async_computation.2 | async-start | bytes 3686400 | tf_op jit(solution)/shard_map/psum | solution.py:74
Sparse Core Ops, SparseCore 0:
  164.7 187.6 reduce-scatter.1
  355.0 117.7 all-reduce.4
where the time goes:
time: 486 us; the launch traced here: 482 us
  waiting for transfers between devices  247 us (51%)
  blocking collectives  120 us (25%)
  local copies, waits for them, and re-layouts  50.9 us (10%)
  matrix products  27.3 us (6%)
  other arithmetic  14.9 us (3%)
  between operations  14.3 us (3%)
  starting transfers between devices  8.37 us (2%)
    reduce_scatter x1, waiting for transfers between devices, shards(): lax.psum_scatter(lax.dot_general(act_cols, grad_rows, (((0,), (0,)), ((),...  188 us
    psum x1, blocking collectives, shards(): dgains = lax.psum(local_gains, ('dp', 'tile'))  64.8 us
    psum x1, waiting for transfers between devices, shards(): dweight = lax.psum(local_grad, 'dp')  55.5 us
    unnamed x30, local copies, waits for them, and re-layouts  24.9 us
    psum x1, blocking collectives, shards(): group_total = lax.psum(jnp.sum(grouped, axis=(0, 1, 3)), 'tile')  22.3 us
    another operation x2, local copies, waits for them, and re-layouts, unfold_channels(): joined = jnp.stack(pieces, axis=-1)  17.6 us
    psum x1, blocking collectives, shards(): lax.psum((jnp.sum(dscaled, axis=(0, 1, 3)), jnp.sum(dscaled * scaled_grou...  17.4 us
    psum x1, blocking collectives, shards(): lax.psum(jnp.sum(centered * centered, axis=(0, 1, 3)), 'tile') / cell_count  15.5 us
  transfers between devices with their start and end apart: 6, of which 3 were waited for; matrix products, arithmetic and copies ran while one was open for 5% of the time, Pallas kernels for 0%

commit v1 on v0

v1 whole, which is shorter than its diff:
```python
import jax
import jax.numpy as jnp
from jax import lax
from jax.experimental import pallas as pl
from jax.experimental.pallas import tpu as pltpu
from jax.sharding import PartitionSpec as P

MESH = pl.DeviceIdType.MESH
BF16 = jnp.bfloat16
F32 = jnp.float32

G = 32
EPSILON = 1e-05
C = 640
PER_GROUP = C // G
ROWS = 8
W = 128
CELLS = ROWS * W
STRIPS = 8
BLOCKS = 45
LANES = 48 * 128
K9 = 9 * C
CI = C // STRIPS
COUNT = float(ROWS * STRIPS * W * PER_GROUP)
SUB = 256


def kernel(
    x_hbm, cot_hbm, mask_ref, w_hbm, gamma_ref, beta_ref,
    df_hbm, dw_hbm, dg_ref,
    x, cot, wpad, cols, wmat, act_t, dn, dwv,
    ms, mr, s1, r1a, r1b, r1c, t2a, t2b, t2c, r2a, r2b, r2c, t3a, t3b, t3c, r3, gat,
    st, sb, gx, gxr, gz, gzr, gc, gcr,
    load_sem, w_sem, out_sem,
    st_send, st_recv, sb_send, sb_recv, halo_send, halo_recv,
    m_send, m_recv,
    a1_send, a1_recv, b1_send, b1_recv, c1_send, c1_recv,
    s2_send, s2_recv, s3_send, s3_recv,
    gat_send, gat_recv, g_send, g_recv,
):
    dp = lax.axis_index("dp")
    tile = lax.axis_index("tile")
    core = lax.rem(dp, 2)
    mx = lax.rem(lax.div(dp, 2), 4)
    zlo = lax.div(dp, 8)
    zhi = lax.div(tile, 4)
    my = lax.rem(tile, 4)
    mz = zhi * 2 + zlo
    mate = 1 - core

    def place(px, py, pz, pc):
        return {
            "dp": (lax.rem(pz, 2) * 4 + px) * 2 + pc,
            "tile": lax.div(pz, 2) * 4 + py,
        }

    def x_peer(d):
        return lax.rem(mx + d, 4)

    def y_peer(d):
        return lax.rem(my + d, 4)

    def z_peer(d):
        return lax.rem(mz + d, 4)

    def remote(src, dst, send, recv, device):
        return pltpu.make_async_remote_copy(
            src_ref=src, dst_ref=dst, send_sem=send, recv_sem=recv, device_id=device, device_id_type=MESH
        )

    on_x = [place(x_peer(d), my, mz, core) for d in (1, 2, 3)]
    on_y = [place(mx, y_peer(d), mz, core) for d in (1, 2, 3)]
    on_z = [place(mx, my, z_peer(d), core) for d in (1, 2, 3)]
    on_core = place(mx, my, mz, mate)
    on_zlo = place(mx, my, zhi * 2 + 1 - zlo, core)

    def on_tile(d):
        return {"dp": dp, "tile": lax.rem(tile + d, STRIPS)}

    load_x = pltpu.make_async_copy(x_hbm.at[0], x, load_sem.at[0])
    load_x.start()
    load_cot = pltpu.make_async_copy(cot_hbm.at[0], cot, load_sem.at[1])
    load_cot.start()
    loads_w = [
        pltpu.make_async_copy(w_hbm.at[k // 3, k % 3], wmat.at[:, k * C : (k + 1) * C], w_sem.at[k]) for k in range(9)
    ]
    for load in loads_w:
        load.start()

    barrier = pltpu.get_barrier_semaphore()
    for device in on_x + on_y + on_z + [on_core]:
        pl.semaphore_signal(barrier, inc=1, device_id=device, device_id_type=MESH)
    for d in (1, 2, 3):
        other = place(mx, y_peer(d), (1 - zhi) * 2 + zlo, core)
        pl.semaphore_signal(barrier, inc=1, device_id=other, device_id_type=MESH)

    load_x.wait()

    def add_rows(i, total):
        return total + jnp.sum(x[i].astype(F32), axis=0, keepdims=True)

    total = lax.fori_loop(0, ROWS, add_rows, jnp.zeros((1, C), F32))
    local_mean = total * (1.0 / CELLS)

    def add_squares(i, sq):
        centered = x[i].astype(F32) - local_mean
        return sq + jnp.sum(centered * centered, axis=0, keepdims=True)

    squares = lax.fori_loop(0, ROWS, add_squares, jnp.zeros((1, C), F32))
    row8 = lax.broadcasted_iota(jnp.int32, (8, C), 0)
    st[tile] = jnp.where(row8 == 0, total, jnp.where(row8 == 1, squares, 0.0))
    pl.semaphore_wait(barrier, 13)
    st_copies = [remote(st.at[tile], st.at[tile], st_send.at[d - 1], st_recv.at[d - 1], on_tile(d)) for d in range(1, 8)]
    for copy in st_copies:
        copy.start()

    load_cot.wait()
    factor = (1.0 + mask_ref[...].astype(F32)).T
    for i in range(ROWS):
        wpad[i + 1] = (cot[i].astype(F32) * factor[:, i : i + 1]).astype(BF16)
    halo = [
        remote(wpad.at[ROWS], wpad.at[0], halo_send.at[0], halo_recv.at[0], on_tile(1)),
        remote(wpad.at[1], wpad.at[ROWS + 1], halo_send.at[1], halo_recv.at[1], on_tile(7)),
    ]
    for copy in halo:
        copy.start()

    rowsw = lax.broadcasted_iota(jnp.int32, (W, C), 0)

    def spread(value, r, offsets):
        ahead = jnp.where(rowsw == W - 1, 0.0, pltpu.roll(value, W - 1, 0))
        behind = jnp.where(rowsw == 0, 0.0, pltpu.roll(value, 1, 0))
        for ox, shifted in enumerate((ahead, value, behind)):
            shifted = shifted.astype(BF16)
            for oy in offsets:
                k = oy * 3 + ox
                start = pl.multiple_of((r - 2 + oy) * W, W)
                cols[pl.ds(start, W), k * C : (k + 1) * C] = shifted

    def spread_inner(r, carry):
        spread(wpad[r].astype(F32), r, (0, 1, 2))
        return carry

    lax.fori_loop(2, ROWS, spread_inner, 0)
    spread(wpad[1].astype(F32), 1, (1, 2))
    spread(wpad[ROWS].astype(F32), ROWS, (0, 1))
    cols[:, K9:] = jnp.zeros((CELLS, LANES - K9), BF16)

    for copy in st_copies:
        copy.wait_recv()
    chan = lax.broadcasted_iota(jnp.int32, (C, 128), 0).astype(F32)
    group = lax.broadcasted_iota(jnp.int32, (C, 128), 1).astype(F32)
    member = jnp.where(jnp.floor((chan + 0.5) * (1.0 / PER_GROUP)) == group, 1.0, 0.0)
    chan_t = lax.broadcasted_iota(jnp.int32, (128, C), 1).astype(F32)
    group_t = lax.broadcasted_iota(jnp.int32, (128, C), 0).astype(F32)
    member_t = jnp.where(jnp.floor((chan_t + 0.5) * (1.0 / PER_GROUP)) == group_t, 1.0, 0.0)

    def to_groups(value):
        return jnp.dot(value, member, precision=lax.Precision.HIGHEST, preferred_element_type=F32)

    def to_channels(value):
        return jnp.dot(value, member_t, precision=lax.Precision.HIGHEST, preferred_element_type=F32)

    sums = st[0]
    for i in range(1, STRIPS):
        sums = sums + st[i]
    mean = to_channels(to_groups(sums) * (1.0 / COUNT))[0:1]
    apart = jnp.zeros((8, C), F32)
    for i in range(STRIPS):
        centered = st[i] * (1.0 / CELLS) - mean
        apart = apart + centered * centered
    spread_sq = apart[0:1] * float(CELLS) + sums[1:2]
    variance = to_groups(jnp.broadcast_to(spread_sq, (8, C))) * (1.0 / COUNT)
    inverse = to_channels(lax.rsqrt(variance + EPSILON))[0:1]
    gamma = gamma_ref[...]
    beta = beta_ref[...]

    def activate(i, carry):
        scaled = (x[i].astype(F32) - mean) * inverse
        normed = scaled * gamma + beta
        sig = jax.nn.sigmoid(normed)
        act = normed * sig
        dn[i] = sig * (1.0 + normed * (1.0 - sig))
        act_t[:, pl.ds(pl.multiple_of(i * W, W), W)] = act.T.astype(BF16)
        return carry

    lax.fori_loop(0, ROWS, activate, 0)

    for copy in halo:
        copy.wait_recv()
    spread(jnp.where(tile == 0, 0.0, wpad[0].astype(F32)), 0, (2,))
    spread(jnp.where(tile == STRIPS - 1, 0.0, wpad[ROWS + 1].astype(F32)), ROWS + 1, (0,))

    def half(owner, part, xq):
        lane = pl.multiple_of(((owner * 3 + part) * 4 + xq) * 256, 256)
        return jnp.dot(act_t[...], cols[:, pl.ds(lane, 256)], preferred_element_type=F32)

    def mate_copy(s, part):
        xq = x_peer(s + 1)
        return remote(ms.at[part, xq], mr.at[part, xq], m_send.at[s, part], m_recv.at[s, part], on_core)

    def x_copy(s):
        xq = x_peer(s + 1)
        return remote(s1.at[0, xq], r1a.at[s], a1_send.at[s], a1_recv.at[s], place(xq, my, mz, core))

    def y_copy(s, d):
        xq = x_peer(s + 1)
        src = s1.at[1, xq, :, :, y_peer(d)]
        return remote(src, r1b.at[d - 1, xq], b1_send.at[s, d - 1], b1_recv.at[s, d - 1], on_y[d - 1])

    def z_copy(s, d):
        xq = x_peer(s + 1)
        src = s1.at[2, xq, lax.rem(z_peer(d), 2), lax.div(z_peer(d), 2)]
        return remote(src, r1c.at[d - 1, xq], c1_send.at[s, d - 1], c1_recv.at[s, d - 1], on_z[d - 1])

    def grad_step(s, carry):
        xq = x_peer(s + 1)
        for part in range(3):
            result = half(mate, part, xq)
            for b in range(2):
                ms[part, xq, b] = result[:, b * 128 : (b + 1) * 128].astype(BF16).reshape(2, 4, CI, 128)
            mate_copy(s, part).start()
        for part in range(3):
            result = half(core, part, xq)
            mate_copy(s, part).wait_recv()
            for b in range(2):
                theirs = mr[part, xq, b].astype(F32)
                ours = result[:, b * 128 : (b + 1) * 128].reshape(2, 4, CI, 128)
                s1[part, xq, b] = (ours + theirs).astype(BF16)
            if part == 0:

                @pl.when(s < 3)
                def _():
                    x_copy(s).start()

            for d in (1, 2, 3):
                if part == 1:
                    y_copy(s, d).start()
                if part == 2:
                    z_copy(s, d).start()
        return carry

    lax.fori_loop(0, 4, grad_step, 0)

    for load in loads_w:
        load.wait()

    def dactive_step(i, carry):
        s0, s1_ = carry
        rows = pl.ds(pl.multiple_of(i * SUB, SUB), SUB)
        dact = lax.dot_general(
            cols[rows, :K9], wmat[...], (((1,), (1,)), ((), ())), preferred_element_type=F32
        )
        for j in range(SUB // W):
            r = i * (SUB // W) + j
            dnormed = dact[j * W : (j + 1) * W] * dn[r]
            dn[r] = dnormed
            scaled = (x[r].astype(F32) - mean) * inverse
            s0 = s0 + jnp.sum(dnormed, axis=0, keepdims=True)
            s1_ = s1_ + jnp.sum(dnormed * scaled, axis=0, keepdims=True)
        return s0, s1_

    zero = jnp.zeros((1, C), F32)
    sum0, sum1 = lax.fori_loop(0, CELLS // SUB, dactive_step, (zero, zero))
    sb[tile] = jnp.where(row8 == 0, sum1, jnp.where(row8 == 1, sum0, 0.0))
    sb_copies = [remote(sb.at[tile], sb.at[tile], sb_send.at[d - 1], sb_recv.at[d - 1], on_tile(d)) for d in range(1, 8)]
    for copy in sb_copies:
        copy.start()

    for s in range(3):
        x_copy(s).wait_recv()
    t2a[...] = s1[0, mx].astype(F32) + r1a[0].astype(F32) + r1a[1].astype(F32) + r1a[2].astype(F32)
    a2 = [
        remote(t2a.at[:, :, y_peer(d)], r2a.at[d - 1], s2_send.at[0, d - 1], s2_recv.at[0, d - 1], on_y[d - 1])
        for d in (1, 2, 3)
    ]
    for copy in a2:
        copy.start()
    for s in range(4):
        for d in (1, 2, 3):
            y_copy(s, d).wait_recv()
    for q in range(4):
        t2b[q] = (
            s1[1, q, :, :, my].astype(F32) + r1b[0, q].astype(F32) + r1b[1, q].astype(F32) + r1b[2, q].astype(F32)
        )
    b2 = [
        remote(
            t2b.at[:, lax.rem(z_peer(d), 2), lax.div(z_peer(d), 2)],
            r2b.at[d - 1], s2_send.at[1, d - 1], s2_recv.at[1, d - 1], on_z[d - 1],
        )
        for d in (1, 2, 3)
    ]
    for copy in b2:
        copy.start()
    for s in range(4):
        for d in (1, 2, 3):
            z_copy(s, d).wait_recv()
    for q in range(4):
        t2c[q] = (
            s1[2, q, zlo, zhi].astype(F32) + r1c[0, q].astype(F32) + r1c[1, q].astype(F32) + r1c[2, q].astype(F32)
        )
    c2 = [
        remote(t2c.at[x_peer(d)], r2c.at[d - 1], s2_send.at[2, d - 1], s2_recv.at[2, d - 1], on_x[d - 1])
        for d in (1, 2, 3)
    ]
    for copy in c2:
        copy.start()

    for copy in sb_copies:
        copy.wait_recv()
    gsum = sb[0]
    for i in range(1, STRIPS):
        gsum = gsum + sb[i]
    gx[...] = gsum
    g1 = [remote(gx, gxr.at[d - 1], g_send.at[d - 1], g_recv.at[d - 1], on_x[d - 1]) for d in (1, 2, 3)]
    for copy in g1:
        copy.start()
    moments = to_channels(to_groups(gsum * gamma) * (1.0 / COUNT))
    second = moments[0:1]
    first = moments[1:2]

    def finish(i, carry):
        scaled = (x[i].astype(F32) - mean) * inverse
        grad = inverse * (dn[i] * gamma - first - scaled * second) + wpad[i + 1].astype(F32)
        cot[i] = grad.astype(BF16)
        return carry

    lax.fori_loop(0, ROWS, finish, 0)
    store_df = pltpu.make_async_copy(cot, df_hbm.at[0], out_sem.at[0])
    store_df.start()

    for copy in a2:
        copy.wait_recv()
    t3a[...] = t2a[:, :, my] + r2a[0] + r2a[1] + r2a[2]
    a3 = [
        remote(
            t3a.at[lax.rem(z_peer(d), 2), lax.div(z_peer(d), 2)],
            r3.at[0, d - 1], s3_send.at[0, d - 1], s3_recv.at[0, d - 1], on_z[d - 1],
        )
        for d in (1, 2, 3)
    ]
    for copy in a3:
        copy.start()
    for copy in b2:
        copy.wait_recv()
    t3b[...] = t2b[:, zlo, zhi] + r2b[0] + r2b[1] + r2b[2]
    b3 = [
        remote(t3b.at[x_peer(d)], r3.at[1, d - 1], s3_send.at[1, d - 1], s3_recv.at[1, d - 1], on_x[d - 1])
        for d in (1, 2, 3)
    ]
    for copy in b3:
        copy.start()
    for copy in c2:
        copy.wait_recv()
    t3c[...] = t2c[mx] + r2c[0] + r2c[1] + r2c[2]
    c3 = [
        remote(t3c.at[y_peer(d)], r3.at[2, d - 1], s3_send.at[2, d - 1], s3_recv.at[2, d - 1], on_y[d - 1])
        for d in (1, 2, 3)
    ]
    for copy in c3:
        copy.start()
    for copy in g1:
        copy.wait_recv()
    gz[...] = gx[...] + gxr[0] + gxr[1] + gxr[2]
    g2 = remote(gz, gzr, g_send.at[3], g_recv.at[3], on_zlo)
    g2.start()

    for part, copies in enumerate((a3, b3, c3)):
        for copy in copies:
            copy.wait_recv()
        own = (t3a[zlo, zhi], t3b[mx], t3c[my])[part]
        gat[core, zlo, mx, part] = (own + r3[part, 0] + r3[part, 1] + r3[part, 2]).astype(BF16)

    mine = gat.at[core, zlo, mx]
    k1 = [remote(mine, mine, gat_send.at[d - 1], gat_recv.at[d - 1], on_x[d - 1]) for d in (1, 2, 3)]
    for copy in k1:
        copy.start()
    g2.wait_recv()
    gc[...] = gz[...] + gzr[...]
    g3 = remote(gc, gcr, g_send.at[4], g_recv.at[4], on_core)
    g3.start()
    for copy in k1:
        copy.wait_recv()
    quad = gat.at[core, zlo]
    k2 = remote(quad, quad, gat_send.at[3], gat_recv.at[3], on_zlo)
    k2.start()
    g3.wait_recv()
    dg_ref[...] = (gc[...] + gcr[...])[0:2]
    k2.wait_recv()
    oct_ = gat.at[core]
    k3 = remote(oct_, oct_, gat_send.at[4], gat_recv.at[4], on_core)
    k3.start()
    k3.wait_recv()
    for b in range(BLOCKS):
        c, rest = divmod(b, 24)
        part, rest = divmod(rest, 8)
        xq, zq = divmod(rest, 2)
        k, j = divmod(b, 5)
        dwv[j, pl.ds(k, CI, stride=9), :] = gat[c, zq, xq, part].astype(F32)
    stores = [pltpu.make_async_copy(dwv.at[j], dw_hbm.at[:, j * 128 : (j + 1) * 128], out_sem.at[j + 1]) for j in range(5)]
    for store in stores:
        store.start()

    for copy in st_copies + halo + sb_copies + a2 + b2 + c2 + a3 + b3 + c3 + g1 + [g2, g3] + k1 + [k2, k3]:
        copy.wait_send()

    def drain(s, carry):
        for part in range(3):
            mate_copy(s, part).wait_send()
        for d in (1, 2, 3):
            y_copy(s, d).wait_send()
            z_copy(s, d).wait_send()

        @pl.when(s < 3)
        def _():
            x_copy(s).wait_send()

        return carry

    lax.fori_loop(0, 4, drain, 0)
    store_df.wait()
    for store in stores:
        store.wait()


def shards(features, cotangent, mask, conv_weight, gamma, beta):
    anywhere = pl.BlockSpec(memory_space=pl.ANY)
    vmem = pl.BlockSpec(memory_space=pltpu.VMEM)
    dma = pltpu.SemaphoreType.DMA

    def buf(*shape, dtype=BF16):
        return pltpu.VMEM(shape, dtype)

    panel = (CI, 128)
    return pl.pallas_call(
        kernel,
        out_shape=(
            jax.ShapeDtypeStruct((1, ROWS, W, C), BF16),
            jax.ShapeDtypeStruct((9 * CI, C), F32),
            jax.ShapeDtypeStruct((2, C), F32),
        ),
        in_specs=[anywhere, anywhere, vmem, anywhere, vmem, vmem],
        out_specs=(anywhere, anywhere, vmem),
        scratch_shapes=[
            buf(ROWS, W, C),
            buf(ROWS, W, C),
            buf(ROWS + 2, W, C),
            buf(CELLS, LANES),
            buf(C, K9),
            buf(C, CELLS),
            buf(ROWS, W, C, dtype=F32),
            buf(5, 9 * CI, 128, dtype=F32),
            buf(3, 4, 2, 2, 4, *panel),
            buf(3, 4, 2, 2, 4, *panel),
            buf(3, 4, 2, 2, 4, *panel),
            buf(3, 2, 2, 4, *panel),
            buf(3, 4, 2, 2, *panel),
            buf(3, 4, 4, *panel),
            buf(2, 2, 4, *panel, dtype=F32),
            buf(4, 2, 2, *panel, dtype=F32),
            buf(4, 4, *panel, dtype=F32),
            buf(3, 2, 2, *panel, dtype=F32),
            buf(3, 4, *panel, dtype=F32),
            buf(3, 4, *panel, dtype=F32),
            buf(2, 2, *panel, dtype=F32),
            buf(4, *panel, dtype=F32),
            buf(4, *panel, dtype=F32),
            buf(3, 3, *panel, dtype=F32),
            buf(2, 2, 4, 3, *panel),
            buf(STRIPS, 8, C, dtype=F32),
            buf(STRIPS, 8, C, dtype=F32),
            buf(8, C, dtype=F32),
            buf(3, 8, C, dtype=F32),
            buf(8, C, dtype=F32),
            buf(8, C, dtype=F32),
            buf(8, C, dtype=F32),
            buf(8, C, dtype=F32),
            dma((2,)),
            dma((9,)),
            dma((6,)),
            dma((7,)),
            dma((7,)),
            dma((7,)),
            dma((7,)),
            dma((2,)),
            dma((2,)),
            dma((4, 3)),
            dma((4, 3)),
            dma((3,)),
            dma((3,)),
            dma((4, 3)),
            dma((4, 3)),
            dma((4, 3)),
            dma((4, 3)),
            dma((3, 3)),
            dma((3, 3)),
            dma((3, 3)),
            dma((3, 3)),
            dma((5,)),
            dma((5,)),
            dma((5,)),
            dma((5,)),
        ],
        compiler_params=pltpu.CompilerParams(
            collective_id=0, has_side_effects=True, vmem_limit_bytes=60 * 1024 * 1024
        ),
        cost_estimate=pl.CostEstimate(flops=4 * CELLS * K9 * C, bytes_accessed=13_000_000, transcendentals=CELLS * C),
    )(features, cotangent, mask[0], conv_weight, gamma[None], beta[None])


def solution(mesh):
    placed = (
        P("dp", "tile", None, None),
        P("dp", "tile", None, None),
        P("dp", "tile", None),
        P(),
        P(),
        P(),
    )
    return jax.shard_map(
        shards,
        mesh=mesh,
        in_specs=placed,
        out_specs=(P("dp", "tile", None, None), P("tile", None), P()),
        check_vma=False,
    )
```

time: 486 us -> 89.9 us (0.18)
  waiting for transfers between devices: 247 us -> 0 us
  blocking collectives: 120 us -> 0 us
  Pallas kernels: 0 us -> 82 us
  local copies, waits for them, and re-layouts: 50.9 us -> 7.01 us
  matrix products: 27.3 us -> 0 us
  other arithmetic: 14.9 us -> 0 us
  between operations: 14.3 us -> 0.65 us
  starting transfers between devices: 8.37 us -> 0 us
    reduce_scatter x1 -> x0, waiting for transfers between devices: 188 us -> none  [shards(): lax.psum_scatter(lax.dot_general(act_cols, grad_rows, (((0,), (0,)), ((),...]
    psum x4 -> x0, blocking collectives: 120 us -> none  [the longest x1 64.8 us: shards(): dgains = lax.psum(local_gains, ('dp', 'tile'))]
    pallas_call x0 -> x1, Pallas kernels: none -> 82 us  [shards(): pl.pallas_call(kernel, out_shape=(jax.ShapeDtypeStruct((1, ROWS, W, C), B...]
    psum x1 -> x0, waiting for transfers between devices: 55.5 us -> none  [shards(): dweight = lax.psum(local_grad, 'dp')]
    dot_general x2 -> x0, matrix products: 27.3 us -> none  [the longest x1 15.3 us: shards(): lax.dot_general(act_cols, grad_rows, (((0,), (0,)), ((), ())), preferred_...]
    unnamed x30 -> x7, local copies, waits for them, and re-layouts: 24.9 us -> 4.48 us
    another operation x4 -> x0, local copies, waits for them, and re-layouts: 17.6 us -> none  [the longest x2 17.6 us: unfold_channels(): joined = jnp.stack(pieces, axis=-1)]
    ppermute x4 -> x0, starting transfers between devices: 8.29 us -> none  [the longest x2 5.71 us: with_halo(): before = lax.ppermute(last, axis, up)]
  transfers between devices with their start and end apart: 6 -> 0, of which waited for: 3 -> 0; matrix products, arithmetic and copies ran while one was open for 5% -> 0% of each run, Pallas kernels for 0% -> 0%
where the time goes in v1:
time: 89.9 us; the launch traced here: 89.7 us
  Pallas kernels  82 us (91%)
  local copies, waits for them, and re-layouts  7.01 us (8%)
    pallas_call x1, Pallas kernels, shards(): pl.pallas_call(kernel, out_shape=(jax.ShapeDtypeStruct((1, ROWS, W, C), B...  82 us
    unnamed x7, local copies, waits for them, and re-layouts  4.48 us

profile of v1, /device:TPU:1, one launch (start us, length us, event | category | flops | bytes accessed | tf_op | source)
XLA Modules:
  0.0 89.7 jit_solution(11438174978329226348)
XLA Ops:
  0.6 1.3 %broadcast_in_dim.6.gamma_ref = f32[1,640]{1,0:T(1,128)} reshape(f32[640]{0:T(1024)} %param.10) | data formatting | bytes 5120 | tf_op jit(solution)/shard_map/broadcast_in_dim | solution.py:508
  1.9 1.3 %broadcast_in_dim.7.beta_ref = f32[1,640]{1,0:T(1,128)} reshape(f32[640]{0:T(1024)} %param.11) | data formatting | bytes 5120 | tf_op jit(solution)/shard_map/broadcast_in_dim | solution.py:508
  3.2 82.0 %shard_map.85 = (bf16[1,8,128,640]{3,2,1,0:T(8,128)(2,1)}, f32[720,640]{1,0:T(8,128)}, f32[2,640]{1,0:T(2,128)}) custom-call(bf16[1,8,128,640]{3,2,1,0:T(8,128)(2,1)} %x_hbm.1, bf16[1,8,128,640]{3,2,1,0:T(8,128)(2,1)} %cot_hbm.1, s32[8,128]{1,0:T(8,128)} %bitcast.1, bf16[3,3,640,640]{3,2,1,0:T(8,128)(2,1)} %w_hbm.1, f32[1,640]{1,0:T(1,128)} %broadcast_in_dim.6.gamma_ref, ...), custom_call_target="tpu_custom_call" | custom-call | flops 15099494400 | bytes 13000000 | tf_op jit(solution)/shard_map/pallas_call | solution.py:435
  85.2 0.0 copy-start
  85.2 2.6 %copy.12 = bf16[1,8,128,640]{3,2,1,0:T(8,128)(2,1)} copy(bf16[1,8,128,640]{3,2,1,0:T(8,128)(2,1)} %get-tuple-element.6) | data formatting | bytes 2621440
  87.9 0.0 copy-done
  87.9 0.0 copy-start.1
  87.9 1.2 %copy.13 = f32[720,640]{1,0:T(8,128)} copy(f32[720,640]{1,0:T(8,128)S(1)} %copy-done) | data formatting | bytes 3686400
  89.1 0.0 copy-done.1
  89.1 0.6 copy.14
Async XLA Ops:
  85.2 2.7 %copy-start = (f32[720,640]{1,0:T(8,128)S(1)}, f32[720,640]{1,0:T(8,128)}, u32[]{:S(2)}) copy-start(f32[720,640]{1,0:T(8,128)} %get-tuple-element.7) | copy-start | bytes 5529604
  87.9 1.2 %copy-start.1 = (f32[2,640]{1,0:T(2,128)S(1)}, f32[2,640]{1,0:T(2,128)}, u32[]{:S(2)}) copy-start(f32[2,640]{1,0:T(2,128)} %get-tuple-element.8) | copy-start | bytes 15364

commit v2 on v1

v2 whole, which is shorter than its diff:
```python
import jax
import jax.numpy as jnp
from jax import lax
from jax.experimental import pallas as pl
from jax.experimental.pallas import tpu as pltpu
from jax.sharding import PartitionSpec as P

MESH = pl.DeviceIdType.MESH
BF16 = jnp.bfloat16
F32 = jnp.float32

G = 32
EPSILON = 1e-05
C = 640
PER_GROUP = C // G
ROWS = 8
W = 128
CELLS = ROWS * W
STRIPS = 8
K3 = 3 * C
LANES = 2048
HALF = LANES // 2
BLOCKS = K3 // 128
K9 = 9 * C
CI = C // STRIPS
COUNT = float(ROWS * STRIPS * W * PER_GROUP)
SUB = 256


def kernel(
    x_hbm, cot_hbm, mask_ref, w_hbm, gamma_ref, beta_ref,
    df, dwv, dg_ref,
    x, cot, wpad, wpad_m, cols, cols_m, wmat, act_t, act_m, dn,
    part_sum, own1, own2, s1, r1a, r1b, r1c, t2a, t2b, t2c, h2a, h2b, h2c, r2a, r2b, r2c, t3a, t3b, t3c, r3, gat,
    st, sb, gx, gxr, gz, gzr, gc, gcr,
    load_sem, w_sem,
    st_send, st_recv, sb_send, sb_recv, halo_send, halo_recv,
    wm_send, wm_recv, am_send, am_recv, hm_send, hm_recv,
    a1_send, a1_recv, b1_send, b1_recv, c1_send, c1_recv,
    s2_send, s2_recv, s3_send, s3_recv,
    gat_send, gat_recv, fwd_send, fwd_recv, g_send, g_recv,
):
    dp = lax.axis_index("dp")
    tile = lax.axis_index("tile")
    core = lax.rem(dp, 2)
    mx = lax.rem(lax.div(dp, 2), 4)
    zlo = lax.div(dp, 8)
    zhi = lax.div(tile, 4)
    my = lax.rem(tile, 4)
    mz = zhi * 2 + zlo
    mate = 1 - core

    def place(px, py, pz, pc):
        return {
            "dp": (lax.rem(pz, 2) * 4 + px) * 2 + pc,
            "tile": lax.div(pz, 2) * 4 + py,
        }

    def x_peer(d):
        return lax.rem(mx + d, 4)

    def y_peer(d):
        return lax.rem(my + d, 4)

    def z_peer(d):
        return lax.rem(mz + d, 4)

    def remote(src, dst, send, recv, device):
        return pltpu.make_async_remote_copy(
            src_ref=src, dst_ref=dst, send_sem=send, recv_sem=recv, device_id=device, device_id_type=MESH
        )

    on_x = [place(x_peer(d), my, mz, core) for d in (1, 2, 3)]
    on_y = [place(mx, y_peer(d), mz, core) for d in (1, 2, 3)]
    on_z = [place(mx, my, z_peer(d), core) for d in (1, 2, 3)]
    on_core = place(mx, my, mz, mate)
    on_zlo = place(mx, my, zhi * 2 + 1 - zlo, core)

    def on_tile(d):
        return {"dp": dp, "tile": lax.rem(tile + d, STRIPS)}

    load_x = pltpu.make_async_copy(x_hbm.at[0], x, load_sem.at[0])
    load_x.start()
    load_cot = pltpu.make_async_copy(cot_hbm.at[0], cot, load_sem.at[1])
    load_cot.start()
    loads_w = [
        pltpu.make_async_copy(w_hbm.at[k // 3, k % 3], wmat.at[:, k * C : (k + 1) * C], w_sem.at[k]) for k in range(9)
    ]

    barrier = pltpu.get_barrier_semaphore()
    for device in on_x + on_y + on_z + [on_core]:
        pl.semaphore_signal(barrier, inc=1, device_id=device, device_id_type=MESH)
    for d in (1, 2, 3):
        other = place(mx, y_peer(d), (1 - zhi) * 2 + zlo, core)
        pl.semaphore_signal(barrier, inc=1, device_id=other, device_id_type=MESH)
        other = place(x_peer(d), my, zhi * 2 + 1 - zlo, core)
        pl.semaphore_signal(barrier, inc=1, device_id=other, device_id_type=MESH)

    load_x.wait()

    def fold(value):
        return jnp.sum(value.reshape(W // 8, 8, C), axis=0)

    zeros8 = jnp.zeros((8, C), F32)
    total = lax.fori_loop(0, ROWS, lambda i, acc: acc + fold(x[i].astype(F32)), zeros8)
    total = jnp.sum(total, axis=0, keepdims=True)
    local_mean = total * (1.0 / CELLS)

    def add_squares(i, acc):
        centered = x[i].astype(F32) - local_mean
        return acc + fold(centered * centered)

    squares = jnp.sum(lax.fori_loop(0, ROWS, add_squares, zeros8), axis=0, keepdims=True)
    st[tile, 0:1] = total
    st[tile, 1:2] = squares
    pl.semaphore_wait(barrier, 16)
    st_copies = [remote(st.at[tile], st.at[tile], st_send.at[d - 1], st_recv.at[d - 1], on_tile(d)) for d in range(1, 8)]
    for copy in st_copies:
        copy.start()

    load_cot.wait()
    for load in loads_w:
        load.start()
    factor = (1.0 + mask_ref[...].astype(F32)).T
    for i in range(ROWS):
        wpad[i + 1] = (cot[i].astype(F32) * factor[:, i : i + 1]).astype(BF16)
    halo = [
        remote(wpad.at[ROWS], wpad.at[0], halo_send.at[0], halo_recv.at[0], on_tile(1)),
        remote(wpad.at[1], wpad.at[ROWS + 1], halo_send.at[1], halo_recv.at[1], on_tile(7)),
    ]
    mate_w = remote(wpad.at[pl.ds(1, ROWS)], wpad_m.at[pl.ds(1, ROWS)], wm_send.at[0], wm_recv.at[0], on_core)
    mate_w.start()
    for copy in halo:
        copy.start()

    rowsw = lax.broadcasted_iota(jnp.int32, (W, C), 0)

    def shifts(value):
        value = value.astype(F32)
        ahead = jnp.where(rowsw == W - 1, 0.0, pltpu.roll(value, W - 1, 0))
        behind = jnp.where(rowsw == 0, 0.0, pltpu.roll(value, 1, 0))
        return ahead.astype(BF16), value.astype(BF16), behind.astype(BF16)

    def spread(r):
        rows = pl.ds(pl.multiple_of(r * W, W), W)
        for ox, shifted in enumerate(shifts(wpad[r])):
            cols[rows, ox * C : (ox + 1) * C] = shifted
        cols[rows, K3:] = jnp.zeros((W, LANES - K3), BF16)

    def spread_mate(r):
        rows = pl.ds(pl.multiple_of(r * W, W), W)
        ahead, middle, behind = shifts(wpad_m[r])
        split = HALF - C

        @pl.when(core == 0)
        def _():
            cols_m[rows, :C] = ahead
            cols_m[rows, C:] = middle[:, :split]

        @pl.when(core == 1)
        def _():
            cols_m[rows, : C - split] = middle[:, split:]
            cols_m[rows, C - split : 2 * C - split] = behind
            cols_m[rows, 2 * C - split :] = jnp.zeros((W, LANES - K3), BF16)

    def inner(step):
        def body(r, carry):
            step(r)
            return carry

        lax.fori_loop(1, ROWS + 1, body, 0)

    inner(spread)

    for copy in st_copies:
        copy.wait_recv()
    chan = lax.broadcasted_iota(jnp.int32, (C, 128), 0).astype(F32)
    group = lax.broadcasted_iota(jnp.int32, (C, 128), 1).astype(F32)
    member = jnp.where(jnp.floor((chan + 0.5) * (1.0 / PER_GROUP)) == group, 1.0, 0.0)
    chan_t = lax.broadcasted_iota(jnp.int32, (128, C), 1).astype(F32)
    group_t = lax.broadcasted_iota(jnp.int32, (128, C), 0).astype(F32)
    member_t = jnp.where(jnp.floor((chan_t + 0.5) * (1.0 / PER_GROUP)) == group_t, 1.0, 0.0)

    def to_groups(value):
        return jnp.dot(value, member, precision=lax.Precision.HIGHEST, preferred_element_type=F32)

    def to_channels(value):
        return jnp.dot(value, member_t, precision=lax.Precision.HIGHEST, preferred_element_type=F32)

    sums = st[0]
    for i in range(1, STRIPS):
        sums = sums + st[i]
    mean = to_channels(to_groups(jnp.broadcast_to(sums[0:1], (8, C))) * (1.0 / COUNT))[0:1]
    apart = jnp.zeros((1, C), F32)
    for i in range(STRIPS):
        centered = st[i, 0:1] * (1.0 / CELLS) - mean
        apart = apart + centered * centered
    spread_sq = apart * float(CELLS) + sums[1:2]
    variance = to_groups(jnp.broadcast_to(spread_sq, (8, C))) * (1.0 / COUNT)
    inverse = to_channels(lax.rsqrt(variance + EPSILON))[0:1]
    gamma = gamma_ref[...].reshape(1, C)
    beta = beta_ref[...].reshape(1, C)

    def mate_act(i):
        block = pl.ds(pl.multiple_of(i * W, W), W)
        return remote(act_t.at[:, block], act_m.at[:, block], am_send.at[i], am_recv.at[i], on_core)

    def activate(i, carry):
        scaled = (x[i].astype(F32) - mean) * inverse
        normed = scaled * gamma + beta
        sig = jax.nn.sigmoid(normed)
        act = normed * sig
        dn[i] = sig * (1.0 + normed * (1.0 - sig))
        act_t[:, pl.ds(pl.multiple_of(i * W, W), W)] = act.T.astype(BF16)
        mate_act(i).start()
        return carry

    lax.fori_loop(0, ROWS, activate, 0)

    for copy in halo:
        copy.wait_recv()

    @pl.when(tile == 0)
    def _():
        wpad[0] = jnp.zeros((W, C), BF16)

    @pl.when(tile == STRIPS - 1)
    def _():
        wpad[ROWS + 1] = jnp.zeros((W, C), BF16)

    mate_edge = [
        remote(wpad.at[r], wpad_m.at[r], hm_send.at[n], hm_recv.at[n], on_core) for n, r in enumerate((0, ROWS + 1))
    ]
    for copy in mate_edge:
        copy.start()
    spread(0)
    spread(ROWS + 1)
    mate_w.wait_recv()
    inner(spread_mate)
    for copy in mate_edge:
        copy.wait_recv()
    spread_mate(0)
    spread_mate(ROWS + 1)
    for i in range(ROWS):
        mate_act(i).wait_recv()

    def partial(part, xq):
        rows = pl.ds((2 - part) * W, CELLS)
        own = cols[rows, pl.ds(pl.multiple_of(core * HALF + xq * 256, 256), 256)]
        theirs = cols_m[rows, pl.ds(pl.multiple_of(xq * 256, 256), 256)]
        return jnp.dot(act_t[...], own, preferred_element_type=F32) + jnp.dot(
            act_m[...], theirs, preferred_element_type=F32
        )

    def turn(s):
        return jnp.where(s == 0, 1, jnp.where(s == 1, 3, jnp.where(s == 2, 2, 0)))

    def x_copy(s):
        xq = x_peer(turn(s))
        return remote(s1.at[0, xq], r1a.at[s], a1_send.at[s], a1_recv.at[s], place(xq, my, mz, core))

    def y_copy(s, d):
        xq = x_peer(turn(s))
        src = s1.at[1, xq, :, :, y_peer(d)]
        return remote(src, r1b.at[d - 1, xq], b1_send.at[s, d - 1], b1_recv.at[s, d - 1], on_y[d - 1])

    def z_copy(s, d):
        xq = x_peer(turn(s))
        src = s1.at[2, xq, lax.rem(z_peer(d), 2), lax.div(z_peer(d), 2)]
        return remote(src, r1c.at[d - 1, xq], c1_send.at[s, d - 1], c1_recv.at[s, d - 1], on_z[d - 1])

    def grad_step(s, carry):
        xq = x_peer(turn(s))
        for part in range(3):
            result = partial(part, xq)
            for b in range(2):
                part_sum[b] = result[:, b * 128 : (b + 1) * 128].reshape(2, 4, CI, 128)
            s1[part, xq] = part_sum[...].astype(BF16)
            if part == 0:

                @pl.when(s < 3)
                def _():
                    x_copy(s).start()

            for d in (1, 3, 2):
                if part == 1:
                    y_copy(s, d).start()
                if part == 2:
                    z_copy(s, d).start()
            if part == 1:
                own1[xq] = part_sum[:, :, my]
            if part == 2:
                own2[xq] = part_sum[zlo, zhi]
            if part == 0:

                @pl.when(s == 3)
                def _():
                    t2a[...] = part_sum[...]
        return carry

    lax.fori_loop(0, 4, grad_step, 0)

    for load in loads_w:
        load.wait()

    def dactive_step(i, carry):
        s0, s1_ = carry
        dact = jnp.zeros((SUB, C), F32)
        for oy in range(3):
            window = cols[pl.ds(pl.multiple_of(i * SUB + (2 - oy) * W, W), SUB), :K3]
            dact = dact + lax.dot_general(
                window, wmat[:, oy * K3 : (oy + 1) * K3], (((1,), (1,)), ((), ())), preferred_element_type=F32
            )
        for j in range(SUB // W):
            r = i * (SUB // W) + j
            dnormed = dact[j * W : (j + 1) * W] * dn[r]
            dn[r] = dnormed
            scaled = (x[r].astype(F32) - mean) * inverse
            s0 = s0 + fold(dnormed)
            s1_ = s1_ + fold(dnormed * scaled)
        return s0, s1_

    sums01 = lax.fori_loop(0, 3, dactive_step, (zeros8, zeros8))

    for s in range(3):
        x_copy(s).wait_recv()
    total = t2a[...] + r1a[0].astype(F32) + r1a[1].astype(F32) + r1a[2].astype(F32)
    t2a[...] = total
    h2a[...] = total.astype(BF16)
    a2 = [
        remote(h2a.at[:, :, y_peer(d)], r2a.at[d - 1], s2_send.at[0, d - 1], s2_recv.at[0, d - 1], on_y[d - 1])
        for d in (1, 2, 3)
    ]
    for copy in a2:
        copy.start()
    for s in range(4):
        for d in (1, 2, 3):
            y_copy(s, d).wait_recv()
    for q in range(4):
        total = own1[q] + r1b[0, q].astype(F32) + r1b[1, q].astype(F32) + r1b[2, q].astype(F32)
        t2b[q] = total
        h2b[q] = total.astype(BF16)
    b2 = [
        remote(
            h2b.at[:, lax.rem(z_peer(d), 2), lax.div(z_peer(d), 2)],
            r2b.at[d - 1], s2_send.at[1, d - 1], s2_recv.at[1, d - 1], on_z[d - 1],
        )
        for d in (1, 2, 3)
    ]
    for copy in b2:
        copy.start()
    for s in range(4):
        for d in (1, 2, 3):
            z_copy(s, d).wait_recv()
    for q in range(4):
        total = own2[q] + r1c[0, q].astype(F32) + r1c[1, q].astype(F32) + r1c[2, q].astype(F32)
        t2c[q] = total
        h2c[q] = total.astype(BF16)
    c2 = [
        remote(h2c.at[x_peer(d)], r2c.at[d - 1], s2_send.at[2, d - 1], s2_recv.at[2, d - 1], on_x[d - 1])
        for d in (1, 2, 3)
    ]
    for copy in c2:
        copy.start()

    sums01 = dactive_step(3, sums01)
    sum0 = jnp.sum(sums01[0], axis=0, keepdims=True)
    sum1 = jnp.sum(sums01[1], axis=0, keepdims=True)
    sb[tile, 0:1] = sum1
    sb[tile, 1:2] = sum0
    sb_copies = [remote(sb.at[tile], sb.at[tile], sb_send.at[d - 1], sb_recv.at[d - 1], on_tile(d)) for d in range(1, 8)]
    for copy in sb_copies:
        copy.start()

    for copy in sb_copies:
        copy.wait_recv()
    gsum = sb[0]
    for i in range(1, STRIPS):
        gsum = gsum + sb[i]
    gx[...] = gsum
    g1 = [remote(gx, gxr.at[d - 1], g_send.at[d - 1], g_recv.at[d - 1], on_x[d - 1]) for d in (1, 2, 3)]
    for copy in g1:
        copy.start()
    weighed = gsum * gamma
    row8 = lax.broadcasted_iota(jnp.int32, (8, C), 0)
    weighed = jnp.where(row8 == 0, weighed[0:1], weighed[1:2])
    moments = to_channels(to_groups(weighed) * (1.0 / COUNT))
    second = moments[0:1]
    first = moments[1:2]

    def finish(i, carry):
        scaled = (x[i].astype(F32) - mean) * inverse
        grad = inverse * (dn[i] * gamma - first - scaled * second) + wpad[i + 1].astype(F32)
        df[0, i] = grad.astype(BF16)
        return carry

    lax.fori_loop(0, ROWS, finish, 0)

    for copy in a2:
        copy.wait_recv()
    t3a[...] = t2a[:, :, my] + r2a[0].astype(F32) + r2a[1].astype(F32) + r2a[2].astype(F32)
    a3 = [
        remote(
            t3a.at[lax.rem(z_peer(d), 2), lax.div(z_peer(d), 2)],
            r3.at[0, d - 1], s3_send.at[0, d - 1], s3_recv.at[0, d - 1], on_z[d - 1],
        )
        for d in (1, 2, 3)
    ]
    for copy in a3:
        copy.start()
    for copy in b2:
        copy.wait_recv()
    t3b[...] = t2b[:, zlo, zhi] + r2b[0].astype(F32) + r2b[1].astype(F32) + r2b[2].astype(F32)
    b3 = [
        remote(t3b.at[x_peer(d)], r3.at[1, d - 1], s3_send.at[1, d - 1], s3_recv.at[1, d - 1], on_x[d - 1])
        for d in (1, 2, 3)
    ]
    for copy in b3:
        copy.start()
    for copy in c2:
        copy.wait_recv()
    t3c[...] = t2c[mx] + r2c[0].astype(F32) + r2c[1].astype(F32) + r2c[2].astype(F32)
    c3 = [
        remote(t3c.at[y_peer(d)], r3.at[2, d - 1], s3_send.at[2, d - 1], s3_recv.at[2, d - 1], on_y[d - 1])
        for d in (1, 2, 3)
    ]
    for copy in c3:
        copy.start()
    for copy in g1:
        copy.wait_recv()
    gz[...] = gx[...] + gxr[0] + gxr[1] + gxr[2]
    g2 = remote(gz, gzr, g_send.at[3], g_recv.at[3], on_zlo)
    g2.start()

    for part, copies in enumerate((a3, b3, c3)):
        for copy in copies:
            copy.wait_recv()
        own = (t3a[zlo, zhi], t3b[mx], t3c[my])[part]
        gat[core, zlo, mx, part] = (own + r3[part, 0] + r3[part, 1] + r3[part, 2]).astype(BF16)

    def piece(dz, dx):
        return gat.at[core, lax.rem(zlo + dz, 2), lax.rem(mx + 4 - dx, 4)]

    def gat_copy(dz, dx):
        mine = gat.at[core, zlo, mx]
        target = place(x_peer(dx), my, zhi * 2 + lax.rem(zlo + dz, 2), core)
        return remote(mine, mine, gat_send.at[dz * 4 + dx], gat_recv.at[dz * 4 + dx], target)

    def mate_gat(dz, dx):
        block = piece(dz, dx)
        return remote(block, block, fwd_send.at[dz * 4 + dx], fwd_recv.at[dz * 4 + dx], on_core)

    def assemble(c, dz, dx):
        zq = lax.rem(zlo + dz, 2)
        xq = lax.rem(mx + 4 - dx, 4)
        for part in range(3):
            b = c * 8 + xq * 2 + zq

            @pl.when(b < BLOCKS)
            def _():
                k = part * 3 + lax.div(b, 5)
                j = lax.rem(b, 5)
                dwv[j, pl.ds(k, CI, stride=9), :] = gat[c, zq, xq, part].astype(F32)

    order = ((0, 0), (0, 1), (0, 3), (1, 0), (0, 2), (1, 1), (1, 3), (1, 2))
    for dz, dx in order[1:]:
        gat_copy(dz, dx).start()
    mate_gat(0, 0).start()
    assemble(core, 0, 0)
    g2.wait_recv()
    gc[...] = gz[...] + gzr[...]
    g3 = remote(gc, gcr, g_send.at[4], g_recv.at[4], on_core)
    g3.start()
    for n, (dz, dx) in enumerate(order[1:]):
        gat_copy(dz, dx).wait_recv()
        mate_gat(dz, dx).start()
        assemble(core, dz, dx)
        mate_gat(*order[n]).wait_recv()
        assemble(mate, *order[n])
    g3.wait_recv()
    dg_ref[...] = gc[...] + gcr[...]
    mate_gat(*order[7]).wait_recv()
    assemble(mate, *order[7])

    for copy in st_copies + halo + [mate_w] + mate_edge + sb_copies + a2 + b2 + c2 + a3 + b3 + c3 + g1 + [g2, g3]:
        copy.wait_send()
    for dz, dx in order:
        mate_gat(dz, dx).wait_send()
        if (dz, dx) != (0, 0):
            gat_copy(dz, dx).wait_send()

    def drain(s, carry):
        mate_act(s * 2).wait_send()
        mate_act(s * 2 + 1).wait_send()
        for d in (1, 2, 3):
            y_copy(s, d).wait_send()
            z_copy(s, d).wait_send()

        @pl.when(s < 3)
        def _():
            x_copy(s).wait_send()

        return carry

    lax.fori_loop(0, 4, drain, 0)


def shards(features, cotangent, mask, conv_weight, gamma, beta):
    anywhere = pl.BlockSpec(memory_space=pl.ANY)
    vmem = pl.BlockSpec(memory_space=pltpu.VMEM)
    dma = pltpu.SemaphoreType.DMA

    def buf(*shape, dtype=BF16):
        return pltpu.VMEM(shape, dtype)

    panel = (CI, 128)
    dfeatures, dweight, dgains = pl.pallas_call(
        kernel,
        out_shape=(
            buf(1, ROWS, W, C),
            buf(5, 9 * CI, 128, dtype=F32),
            buf(2, C, dtype=F32),
        ),
        in_specs=[anywhere, anywhere, vmem, anywhere, vmem, vmem],
        out_specs=(vmem, vmem, vmem),
        scratch_shapes=[
            buf(ROWS, W, C),
            buf(ROWS, W, C),
            buf(ROWS + 2, W, C),
            buf(ROWS + 2, W, C),
            buf(CELLS + 2 * W, LANES),
            buf(CELLS + 2 * W, HALF),
            buf(C, K9),
            buf(C, CELLS),
            buf(C, CELLS),
            buf(ROWS, W, C, dtype=F32),
            buf(2, 2, 4, *panel, dtype=F32),
            buf(4, 2, 2, *panel, dtype=F32),
            buf(4, 4, *panel, dtype=F32),
            buf(3, 4, 2, 2, 4, *panel),
            buf(3, 2, 2, 4, *panel),
            buf(3, 4, 2, 2, *panel),
            buf(3, 4, 4, *panel),
            buf(2, 2, 4, *panel, dtype=F32),
            buf(4, 2, 2, *panel, dtype=F32),
            buf(4, 4, *panel, dtype=F32),
            buf(2, 2, 4, *panel),
            buf(4, 2, 2, *panel),
            buf(4, 4, *panel),
            buf(3, 2, 2, *panel),
            buf(3, 4, *panel),
            buf(3, 4, *panel),
            buf(2, 2, *panel, dtype=F32),
            buf(4, *panel, dtype=F32),
            buf(4, *panel, dtype=F32),
            buf(3, 3, *panel, dtype=F32),
            buf(2, 2, 4, 3, *panel),
            buf(STRIPS, 2, C, dtype=F32),
            buf(STRIPS, 2, C, dtype=F32),
            buf(2, C, dtype=F32),
            buf(3, 2, C, dtype=F32),
            buf(2, C, dtype=F32),
            buf(2, C, dtype=F32),
            buf(2, C, dtype=F32),
            buf(2, C, dtype=F32),
            dma((2,)),
            dma((9,)),
            dma((7,)),
            dma((7,)),
            dma((7,)),
            dma((7,)),
            dma((2,)),
            dma((2,)),
            dma((1,)),
            dma((1,)),
            dma((ROWS,)),
            dma((ROWS,)),
            dma((2,)),
            dma((2,)),
            dma((3,)),
            dma((3,)),
            dma((4, 3)),
            dma((4, 3)),
            dma((4, 3)),
            dma((4, 3)),
            dma((3, 3)),
            dma((3, 3)),
            dma((3, 3)),
            dma((3, 3)),
            dma((8,)),
            dma((8,)),
            dma((8,)),
            dma((8,)),
            dma((5,)),
            dma((5,)),
        ],
        compiler_params=pltpu.CompilerParams(
            collective_id=0, has_side_effects=True, vmem_limit_bytes=56 * 1024 * 1024
        ),
        cost_estimate=pl.CostEstimate(flops=4 * CELLS * K9 * C, bytes_accessed=13_000_000, transcendentals=CELLS * C),
    )(features, cotangent, mask[0], conv_weight, gamma, beta)
    return dfeatures, jnp.concatenate([dweight[j] for j in range(5)], axis=1), dgains


def solution(mesh):
    placed = (
        P("dp", "tile", None, None),
        P("dp", "tile", None, None),
        P("dp", "tile", None),
        P(),
        P(),
        P(),
    )
    return jax.shard_map(
        shards,
        mesh=mesh,
        in_specs=placed,
        out_specs=(P("dp", "tile", None, None), P("tile", None), P()),
        check_vma=False,
    )
```

time: 89.9 us -> 71.7 us (0.80)
  Pallas kernels: 82 us -> 67.8 us
  local copies, waits for them, and re-layouts: 7.01 us -> 3.01 us
    pallas_call x1, Pallas kernels: 82 us -> 67.8 us  [shards(): pl.pallas_call(kernel, out_shape=(buf(1, ROWS, W, C), buf(5, 9 * CI, 128,...]
    broadcast_in_dim x2 -> x0, local copies, waits for them, and re-layouts: 2.53 us -> none  [the longest x1 1.27 us: shards(): gamma[None]]
    unnamed x7 -> x8, local copies, waits for them, and re-layouts: 4.48 us -> 2.98 us
where the time goes in v2:
time: 71.7 us; the launch traced here: 71.5 us
  Pallas kernels  67.8 us (95%)
  local copies, waits for them, and re-layouts  3.01 us (4%)
    pallas_call x1, Pallas kernels, shards(): pl.pallas_call(kernel, out_shape=(buf(1, ROWS, W, C), buf(5, 9 * CI, 128,...  67.8 us
    unnamed x8, local copies, waits for them, and re-layouts  2.98 us

profile of v2, /device:TPU:1, one launch (start us, length us, event | category | flops | bytes accessed | tf_op | source)
XLA Modules:
  0.0 71.5 jit_solution(13357923989876218143)
XLA Ops:
  0.6 67.8 %shard_map.85 = (bf16[1,8,128,640]{3,2,1,0:T(8,128)(2,1)S(1)}, f32[5,720,128]{2,1,0:T(8,128)S(1)}, f32[2,640]{1,0:T(2,128)S(1)}) custom-call(bf16[1,8,128,640]{3,2,1,0:T(8,128)(2,1)} %x_hbm.1, bf16[1,8,128,640]{3,2,1,0:T(8,128)(2,1)} %cot_hbm.1, s32[8,128]{1,0:T(8,128)} %bitcast.11, bf16[3,3,640,640]{3,2,1,0:T(8,128)(2,1)} %w_hbm.1, f32[640]{0:T(1024)} %gamma_ref.1, ...), custom_call_target="tpu_custom_call" | custom-call | flops 15099494400 | bytes 13000000 | tf_op jit(solution)/shard_map/pallas_call | solution.py:517
  68.5 1.1 %copy.15 = bf16[1,8,128,640]{3,2,1,0:T(8,128)(2,1)} copy(bf16[1,8,128,640]{3,2,1,0:T(8,128)(2,1)S(1)} %get-tuple-element.9) | data formatting | bytes 2621440
  69.5 0.6 copy.16
  70.3 0.0 copy-start
  70.3 1.2 %copy-done = f32[720,640]{1,0:T(8,128)} copy-done((f32[720,640]{1,0:T(8,128)}, f32[720,640]{1,0:T(8,128)S(1)}, u32[]{:S(2)}) %copy-start) | copy-done | bytes 1843224
  (5 shorter events, 0.1 us)
Async XLA Ops:
  70.3 1.2 %copy-start = (f32[720,640]{1,0:T(8,128)}, f32[720,640]{1,0:T(8,128)S(1)}, u32[]{:S(2)}) copy-start(f32[720,640]{1,0:T(8,128)S(1)} %bitcast_dynamic-update-slice_fusion) | copy-start | bytes 5529604

commit v3 on v2

--- a/solution.py
+++ b/solution.py
@@ -37,7 +37,7 @@
     st_send, st_recv, sb_send, sb_recv, halo_send, halo_recv,
     wm_send, wm_recv, am_send, am_recv, hm_send, hm_recv,
     a1_send, a1_recv, b1_send, b1_recv, c1_send, c1_recv,
-    s2_send, s2_recv, s3_send, s3_recv,
+    a2_send, a2_recv, b2_send, b2_recv, c2_send, c2_recv, s3_send, s3_recv,
     gat_send, gat_recv, fwd_send, fwd_recv, g_send, g_recv,
 ):
     dp = lax.axis_index("dp")
@@ -208,7 +208,7 @@
     def activate(i, carry):
         scaled = (x[i].astype(F32) - mean) * inverse
         normed = scaled * gamma + beta
-        sig = jax.nn.sigmoid(normed)
+        sig = 0.5 + 0.5 * jnp.tanh(0.5 * normed)
         act = normed * sig
         dn[i] = sig * (1.0 + normed * (1.0 - sig))
         act_t[:, pl.ds(pl.multiple_of(i * W, W), W)] = act.T.astype(BF16)
@@ -274,8 +274,9 @@
         for part in range(3):
             result = partial(part, xq)
             for b in range(2):
-                part_sum[b] = result[:, b * 128 : (b + 1) * 128].reshape(2, 4, CI, 128)
-            s1[part, xq] = part_sum[...].astype(BF16)
+                piece = result[:, b * 128 : (b + 1) * 128].reshape(2, 4, CI, 128)
+                part_sum[b] = piece
+                s1[part, xq, b] = piece.astype(BF16)
             if part == 0:
 
                 @pl.when(s < 3)
@@ -320,49 +321,68 @@
             s1_ = s1_ + fold(dnormed * scaled)
         return s0, s1_
 
-    sums01 = lax.fori_loop(0, 3, dactive_step, (zeros8, zeros8))
-
-    for s in range(3):
-        x_copy(s).wait_recv()
-    total = t2a[...] + r1a[0].astype(F32) + r1a[1].astype(F32) + r1a[2].astype(F32)
-    t2a[...] = total
-    h2a[...] = total.astype(BF16)
-    a2 = [
-        remote(h2a.at[:, :, y_peer(d)], r2a.at[d - 1], s2_send.at[0, d - 1], s2_recv.at[0, d - 1], on_y[d - 1])
-        for d in (1, 2, 3)
-    ]
-    for copy in a2:
-        copy.start()
-    for s in range(4):
+    def z_of(d):
+        return lax.rem(z_peer(d), 2), lax.div(z_peer(d), 2)
+
+    def b2_copy(i, d):
+        xq = x_peer(turn(i))
+        zq, zh = z_of(d)
+        return remote(h2b.at[xq, zq, zh], r2b.at[d - 1, xq], b2_send.at[i, d - 1], b2_recv.at[i, d - 1], on_z[d - 1])
+
+    def c2_copy(i):
+        xq = x_peer(turn(i))
+        return remote(h2c.at[xq], r2c.at[i], c2_send.at[i], c2_recv.at[i], place(xq, my, mz, core))
+
+    def a2_copy(n, d):
+        zq, zh = z_of(n)
+        return remote(h2a.at[zq, zh, y_peer(d)], r2a.at[d - 1, n], a2_send.at[n, d - 1], a2_recv.at[n, d - 1], on_y[d - 1])
+
+    def a3_copy(d):
+        zq, zh = z_of(d)
+        return remote(t3a.at[zq, zh], r3.at[0, d - 1], s3_send.at[0, d - 1], s3_recv.at[0, d - 1], on_z[d - 1])
+
+    def b3_copy(d):
+        return remote(t3b.at[x_peer(d)], r3.at[1, d - 1], s3_send.at[1, d - 1], s3_recv.at[1, d - 1], on_x[d - 1])
+
+    def c3_copy(d):
+        return remote(t3c.at[y_peer(d)], r3.at[2, d - 1], s3_send.at[2, d - 1], s3_recv.at[2, d - 1], on_y[d - 1])
+
+    def first_bc(i):
+        xq = x_peer(turn(i))
         for d in (1, 2, 3):
-            y_copy(s, d).wait_recv()
-    for q in range(4):
-        total = own1[q] + r1b[0, q].astype(F32) + r1b[1, q].astype(F32) + r1b[2, q].astype(F32)
-        t2b[q] = total
-        h2b[q] = total.astype(BF16)
-    b2 = [
-        remote(
-            h2b.at[:, lax.rem(z_peer(d), 2), lax.div(z_peer(d), 2)],
-            r2b.at[d - 1], s2_send.at[1, d - 1], s2_recv.at[1, d - 1], on_z[d - 1],
-        )
-        for d in (1, 2, 3)
-    ]
-    for copy in b2:
-        copy.start()
-    for s in range(4):
+            y_copy(i, d).wait_recv()
+        total = own1[xq] + r1b[0, xq].astype(F32) + r1b[1, xq].astype(F32) + r1b[2, xq].astype(F32)
+        t2b[xq] = total
+        h2b[xq] = total.astype(BF16)
+        for d in (1, 3, 2):
+            b2_copy(i, d).start()
         for d in (1, 2, 3):
-            z_copy(s, d).wait_recv()
-    for q in range(4):
-        total = own2[q] + r1c[0, q].astype(F32) + r1c[1, q].astype(F32) + r1c[2, q].astype(F32)
-        t2c[q] = total
-        h2c[q] = total.astype(BF16)
-    c2 = [
-        remote(h2c.at[x_peer(d)], r2c.at[d - 1], s2_send.at[2, d - 1], s2_recv.at[2, d - 1], on_x[d - 1])
-        for d in (1, 2, 3)
-    ]
-    for copy in c2:
-        copy.start()
-
+            z_copy(i, d).wait_recv()
+        total = own2[xq] + r1c[0, xq].astype(F32) + r1c[1, xq].astype(F32) + r1c[2, xq].astype(F32)
+        t2c[xq] = total
+        h2c[xq] = total.astype(BF16)
+        if i < 3:
+            c2_copy(i).start()
+
+    def first_a():
+        for i in range(3):
+            x_copy(i).wait_recv()
+        total = t2a[...] + r1a[0].astype(F32) + r1a[1].astype(F32) + r1a[2].astype(F32)
+        t2a[...] = total
+        h2a[...] = total.astype(BF16)
+        for n in (1, 3, 2, 0):
+            for d in (1, 3, 2):
+                a2_copy(n, d).start()
+
+    sums01 = (zeros8, zeros8)
+    sums01 = dactive_step(0, sums01)
+    first_bc(0)
+    sums01 = dactive_step(1, sums01)
+    first_bc(1)
+    first_bc(2)
+    first_a()
+    first_bc(3)
+    sums01 = dactive_step(2, sums01)
     sums01 = dactive_step(3, sums01)
     sum0 = jnp.sum(sums01[0], axis=0, keepdims=True)
     sum1 = jnp.sum(sums01[1], axis=0, keepdims=True)
@@ -371,6 +391,29 @@
     sb_copies = [remote(sb.at[tile], sb.at[tile], sb_send.at[d - 1], sb_recv.at[d - 1], on_tile(d)) for d in range(1, 8)]
     for copy in sb_copies:
         copy.start()
+
+    for i, n in ((0, 1), (1, 3), (2, 2), (3, 0)):
+        xq = x_peer(n)
+        for d in (1, 2, 3):
+            b2_copy(i, d).wait_recv()
+        t3b[xq] = (
+            t2b[xq, zlo, zhi] + r2b[0, xq].astype(F32) + r2b[1, xq].astype(F32) + r2b[2, xq].astype(F32)
+        )
+        if n:
+            b3_copy(n).start()
+        zq, zh = z_of(n)
+        for d in (1, 2, 3):
+            a2_copy(n, d).wait_recv()
+        t3a[zq, zh] = (
+            t2a[zq, zh, my] + r2a[0, n].astype(F32) + r2a[1, n].astype(F32) + r2a[2, n].astype(F32)
+        )
+        if n:
+            a3_copy(n).start()
+    for i in range(3):
+        c2_copy(i).wait_recv()
+    t3c[...] = t2c[mx] + r2c[0].astype(F32) + r2c[1].astype(F32) + r2c[2].astype(F32)
+    for d in (1, 3, 2):
+        c3_copy(d).start()
 
     for copy in sb_copies:
         copy.wait_recv()
@@ -381,6 +424,38 @@
     g1 = [remote(gx, gxr.at[d - 1], g_send.at[d - 1], g_recv.at[d - 1], on_x[d - 1]) for d in (1, 2, 3)]
     for copy in g1:
         copy.start()
+
+    order = ((0, 1), (0, 3), (1, 0), (0, 2), (1, 1), (1, 3), (1, 2))
+
+    def gat_copy(part, dz, dx):
+        mine = gat.at[core, zlo, mx, part]
+        target = place(x_peer(dx), my, zhi * 2 + lax.rem(zlo + dz, 2), core)
+        return remote(mine, mine, gat_send.at[part, dz * 4 + dx], gat_recv.at[part, dz * 4 + dx], target)
+
+    def mate_gat(part, dz, dx):
+        block = gat.at[core, lax.rem(zlo + dz, 2), lax.rem(mx + 4 - dx, 4), part]
+        return remote(block, block, fwd_send.at[part, dz * 4 + dx], fwd_recv.at[part, dz * 4 + dx], on_core)
+
+    def assemble(c, part, dz, dx):
+        zq = lax.rem(zlo + dz, 2)
+        xq = lax.rem(mx + 4 - dx, 4)
+        b = c * 8 + xq * 2 + zq
+
+        @pl.when(b < BLOCKS)
+        def _():
+            k = part * 3 + lax.div(b, 5)
+            j = lax.rem(b, 5)
+            dwv[j, pl.ds(k, CI, stride=9), :] = gat[c, zq, xq, part].astype(F32)
+
+    for part, third in ((1, b3_copy), (0, a3_copy), (2, c3_copy)):
+        for d in (1, 2, 3):
+            third(d).wait_recv()
+        own = (t3a[zlo, zhi], t3b[mx], t3c[my])[part]
+        gat[core, zlo, mx, part] = (own + r3[part, 0] + r3[part, 1] + r3[part, 2]).astype(BF16)
+        for dz, dx in order:
+            gat_copy(part, dz, dx).start()
+        mate_gat(part, 0, 0).start()
+
     weighed = gsum * gamma
     row8 = lax.broadcasted_iota(jnp.int32, (8, C), 0)
     weighed = jnp.where(row8 == 0, weighed[0:1], weighed[1:2])
@@ -388,6 +463,12 @@
     second = moments[0:1]
     first = moments[1:2]
 
+    for copy in g1:
+        copy.wait_recv()
+    gz[...] = gx[...] + gxr[0] + gxr[1] + gxr[2]
+    g2 = remote(gz, gzr, g_send.at[3], g_recv.at[3], on_zlo)
+    g2.start()
+
     def finish(i, carry):
         scaled = (x[i].astype(F32) - mean) * inverse
         grad = inverse * (dn[i] * gamma - first - scaled * second) + wpad[i + 1].astype(F32)
@@ -395,99 +476,36 @@
         return carry
 
     lax.fori_loop(0, ROWS, finish, 0)
-
-    for copy in a2:
-        copy.wait_recv()
-    t3a[...] = t2a[:, :, my] + r2a[0].astype(F32) + r2a[1].astype(F32) + r2a[2].astype(F32)
-    a3 = [
-        remote(
-            t3a.at[lax.rem(z_peer(d), 2), lax.div(z_peer(d), 2)],
-            r3.at[0, d - 1], s3_send.at[0, d - 1], s3_recv.at[0, d - 1], on_z[d - 1],
-        )
-        for d in (1, 2, 3)
-    ]
-    for copy in a3:
-        copy.start()
-    for copy in b2:
-        copy.wait_recv()
-    t3b[...] = t2b[:, zlo, zhi] + r2b[0].astype(F32) + r2b[1].astype(F32) + r2b[2].astype(F32)
-    b3 = [
-        remote(t3b.at[x_peer(d)], r3.at[1, d - 1], s3_send.at[1, d - 1], s3_recv.at[1, d - 1], on_x[d - 1])
-        for d in (1, 2, 3)
-    ]
-    for copy in b3:
-        copy.start()
-    for copy in c2:
-        copy.wait_recv()
-    t3c[...] = t2c[mx] + r2c[0].astype(F32) + r2c[1].astype(F32) + r2c[2].astype(F32)
-    c3 = [
-        remote(t3c.at[y_peer(d)], r3.at[2, d - 1], s3_send.at[2, d - 1], s3_recv.at[2, d - 1], on_y[d - 1])
-        for d in (1, 2, 3)
-    ]
-    for copy in c3:
-        copy.start()
-    for copy in g1:
-        copy.wait_recv()
-    gz[...] = gx[...] + gxr[0] + gxr[1] + gxr[2]
-    g2 = remote(gz, gzr, g_send.at[3], g_recv.at[3], on_zlo)
-    g2.start()
-
-    for part, copies in enumerate((a3, b3, c3)):
-        for copy in copies:
-            copy.wait_recv()
-        own = (t3a[zlo, zhi], t3b[mx], t3c[my])[part]
-        gat[core, zlo, mx, part] = (own + r3[part, 0] + r3[part, 1] + r3[part, 2]).astype(BF16)
-
-    def piece(dz, dx):
-        return gat.at[core, lax.rem(zlo + dz, 2), lax.rem(mx + 4 - dx, 4)]
-
-    def gat_copy(dz, dx):
-        mine = gat.at[core, zlo, mx]
-        target = place(x_peer(dx), my, zhi * 2 + lax.rem(zlo + dz, 2), core)
-        return remote(mine, mine, gat_send.at[dz * 4 + dx], gat_recv.at[dz * 4 + dx], target)
-
-    def mate_gat(dz, dx):
-        block = piece(dz, dx)
-        return remote(block, block, fwd_send.at[dz * 4 + dx], fwd_recv.at[dz * 4 + dx], on_core)
-
-    def assemble(c, dz, dx):
-        zq = lax.rem(zlo + dz, 2)
-        xq = lax.rem(mx + 4 - dx, 4)
-        for part in range(3):
-            b = c * 8 + xq * 2 + zq
-
-            @pl.when(b < BLOCKS)
-            def _():
-                k = part * 3 + lax.div(b, 5)
-                j = lax.rem(b, 5)
-                dwv[j, pl.ds(k, CI, stride=9), :] = gat[c, zq, xq, part].astype(F32)
-
-    order = ((0, 0), (0, 1), (0, 3), (1, 0), (0, 2), (1, 1), (1, 3), (1, 2))
-    for dz, dx in order[1:]:
-        gat_copy(dz, dx).start()
-    mate_gat(0, 0).start()
-    assemble(core, 0, 0)
     g2.wait_recv()
     gc[...] = gz[...] + gzr[...]
     g3 = remote(gc, gcr, g_send.at[4], g_recv.at[4], on_core)
     g3.start()
-    for n, (dz, dx) in enumerate(order[1:]):
-        gat_copy(dz, dx).wait_recv()
-        mate_gat(dz, dx).start()
-        assemble(core, dz, dx)
-        mate_gat(*order[n]).wait_recv()
-        assemble(mate, *order[n])
+
+    for part in (1, 0, 2):
+        assemble(core, part, 0, 0)
+    for dz, dx in order:
+        for part in (1, 0, 2):
+            gat_copy(part, dz, dx).wait_recv()
+            mate_gat(part, dz, dx).start()
+            assemble(core, part, dz, dx)
     g3.wait_recv()
     dg_ref[...] = gc[...] + gcr[...]
-    mate_gat(*order[7]).wait_recv()
-    assemble(mate, *order[7])
-
-    for copy in st_copies + halo + [mate_w] + mate_edge + sb_copies + a2 + b2 + c2 + a3 + b3 + c3 + g1 + [g2, g3]:
+    for dz, dx in ((0, 0),) + order:
+        for part in (1, 0, 2):
+            mate_gat(part, dz, dx).wait_recv()
+            assemble(mate, part, dz, dx)
+
+    for copy in st_copies + halo + [mate_w] + mate_edge + sb_copies + g1 + [g2, g3]:
         copy.wait_send()
-    for dz, dx in order:
-        mate_gat(dz, dx).wait_send()
-        if (dz, dx) != (0, 0):
-            gat_copy(dz, dx).wait_send()
+    for part in range(3):
+        mate_gat(part, 0, 0).wait_send()
+        for dz, dx in order:
+            gat_copy(part, dz, dx).wait_send()
+            mate_gat(part, dz, dx).wait_send()
+    for d in (1, 2, 3):
+        a3_copy(d).wait_send()
+        b3_copy(d).wait_send()
+        c3_copy(d).wait_send()
 
     def drain(s, carry):
         mate_act(s * 2).wait_send()
@@ -495,10 +513,13 @@
         for d in (1, 2, 3):
             y_copy(s, d).wait_send()
             z_copy(s, d).wait_send()
+            a2_copy(s, d).wait_send()
+            b2_copy(s, d).wait_send()
 
         @pl.when(s < 3)
         def _():
             x_copy(s).wait_send()
+            c2_copy(s).wait_send()
 
         return carry
 
@@ -547,7 +568,7 @@
             buf(2, 2, 4, *panel),
             buf(4, 2, 2, *panel),
             buf(4, 4, *panel),
-            buf(3, 2, 2, *panel),
+            buf(3, 4, *panel),
             buf(3, 4, *panel),
             buf(3, 4, *panel),
             buf(2, 2, *panel, dtype=F32),
@@ -583,14 +604,18 @@
             dma((4, 3)),
             dma((4, 3)),
             dma((4, 3)),
+            dma((4, 3)),
+            dma((4, 3)),
+            dma((4, 3)),
+            dma((4, 3)),
+            dma((3,)),
+            dma((3,)),
             dma((3, 3)),
             dma((3, 3)),
-            dma((3, 3)),
-            dma((3, 3)),
-            dma((8,)),
-            dma((8,)),
-            dma((8,)),
-            dma((8,)),
+            dma((3, 8)),
+            dma((3, 8)),
+            dma((3, 8)),
+            dma((3, 8)),
             dma((5,)),
             dma((5,)),
         ],

time: 71.7 us -> 67.5 us (0.941)
  Pallas kernels: 67.8 us -> 63.6 us
    pallas_call x1, Pallas kernels: 67.8 us -> 63.6 us  [shards(): pl.pallas_call(kernel, out_shape=(buf(1, ROWS, W, C), buf(5, 9 * CI, 128,...]
where the time goes in v3:
time: 67.5 us; the launch traced here: 67.3 us
  Pallas kernels  63.6 us (94%)
  local copies, waits for them, and re-layouts  3.01 us (4%)
  between operations  0.68 us (1%)
    pallas_call x1, Pallas kernels, shards(): pl.pallas_call(kernel, out_shape=(buf(1, ROWS, W, C), buf(5, 9 * CI, 128,...  63.6 us
    unnamed x8, local copies, waits for them, and re-layouts  2.98 us

profile of v3, /device:TPU:1, one launch (start us, length us, event | category | flops | bytes accessed | tf_op | source)
XLA Modules:
  0.0 67.3 jit_solution(9920030411405666335)
XLA Ops:
  0.6 63.6 %shard_map.85 = (bf16[1,8,128,640]{3,2,1,0:T(8,128)(2,1)S(1)}, f32[5,720,128]{2,1,0:T(8,128)S(1)}, f32[2,640]{1,0:T(2,128)S(1)}) custom-call(bf16[1,8,128,640]{3,2,1,0:T(8,128)(2,1)} %x_hbm.1, bf16[1,8,128,640]{3,2,1,0:T(8,128)(2,1)} %cot_hbm.1, s32[8,128]{1,0:T(8,128)} %bitcast.11, bf16[3,3,640,640]{3,2,1,0:T(8,128)(2,1)} %w_hbm.1, f32[640]{0:T(1024)} %gamma_ref.1, ...), custom_call_target="tpu_custom_call" | custom-call | flops 15099494400 | bytes 13000000 | tf_op jit(solution)/shard_map/pallas_call | solution.py:538
  64.2 1.1 %copy.15 = bf16[1,8,128,640]{3,2,1,0:T(8,128)(2,1)} copy(bf16[1,8,128,640]{3,2,1,0:T(8,128)(2,1)S(1)} %get-tuple-element.9) | data formatting | bytes 2621440
  65.3 0.6 copy.16
  66.1 0.0 copy-start
  66.1 1.2 %copy-done = f32[720,640]{1,0:T(8,128)} copy-done((f32[720,640]{1,0:T(8,128)}, f32[720,640]{1,0:T(8,128)S(1)}, u32[]{:S(2)}) %copy-start) | copy-done | bytes 1843224
  (5 shorter events, 0.1 us)
Async XLA Ops:
  66.1 1.2 %copy-start = (f32[720,640]{1,0:T(8,128)}, f32[720,640]{1,0:T(8,128)S(1)}, u32[]{:S(2)}) copy-start(f32[720,640]{1,0:T(8,128)S(1)} %bitcast_dynamic-update-slice_fusion) | copy-start | bytes 5529604

commit v4 on v3

--- a/solution.py
+++ b/solution.py
@@ -24,13 +24,13 @@
 K9 = 9 * C
 CI = C // STRIPS
 COUNT = float(ROWS * STRIPS * W * PER_GROUP)
-SUB = 256
+SUB = 512
 
 
 def kernel(
-    x_hbm, cot_hbm, mask_ref, w_hbm, gamma_ref, beta_ref,
+    x_hbm, cot_hbm, mask_hbm, w_hbm, gamma_hbm, beta_hbm,
     df, dwv, dg_ref,
-    x, cot, wpad, wpad_m, cols, cols_m, wmat, act_t, act_m, dn,
+    mask_ref, gamma_ref, beta_ref, x, cot, wpad, wpad_m, cols, cols_m, wmat, act_t, act_m, dn,
     part_sum, own1, own2, s1, r1a, r1b, r1c, t2a, t2b, t2c, h2a, h2b, h2c, r2a, r2b, r2c, t3a, t3b, t3c, r3, gat,
     st, sb, gx, gxr, gz, gzr, gc, gcr,
     load_sem, w_sem,
@@ -83,6 +83,11 @@
     load_x.start()
     load_cot = pltpu.make_async_copy(cot_hbm.at[0], cot, load_sem.at[1])
     load_cot.start()
+    load_mask = pltpu.make_async_copy(mask_hbm.at[0], mask_ref, load_sem.at[2])
+    load_gamma = pltpu.make_async_copy(gamma_hbm, gamma_ref, load_sem.at[3])
+    load_beta = pltpu.make_async_copy(beta_hbm, beta_ref, load_sem.at[4])
+    for load in (load_mask, load_gamma, load_beta):
+        load.start()
     loads_w = [
         pltpu.make_async_copy(w_hbm.at[k // 3, k % 3], wmat.at[:, k * C : (k + 1) * C], w_sem.at[k]) for k in range(9)
     ]
@@ -119,6 +124,8 @@
         copy.start()
 
     load_cot.wait()
+    for load in (load_mask, load_gamma, load_beta):
+        load.wait()
     for load in loads_w:
         load.start()
     factor = (1.0 + mask_ref[...].astype(F32)).T
@@ -172,21 +179,30 @@
 
     inner(spread)
 
+    chan = lax.broadcasted_iota(jnp.int32, (C, 128), 0).astype(F32)
+    group = lax.broadcasted_iota(jnp.int32, (C, 128), 1).astype(F32)
+    member = jnp.where(jnp.floor((chan + 0.5) * (1.0 / PER_GROUP)) == group, 1.0, 0.0).astype(BF16)
+    chan_t = lax.broadcasted_iota(jnp.int32, (128, C), 1).astype(F32)
+    group_t = lax.broadcasted_iota(jnp.int32, (128, C), 0).astype(F32)
+    member_t = jnp.where(jnp.floor((chan_t + 0.5) * (1.0 / PER_GROUP)) == group_t, 1.0, 0.0).astype(BF16)
+
+    def in_parts(value):
+        high = value.astype(BF16).astype(F32)
+        middle = (value - high).astype(BF16).astype(F32)
+        return jnp.concatenate([high, middle, value - high - middle], axis=0).astype(BF16)
+
+    def times(value, table):
+        product = jnp.dot(in_parts(value), table, preferred_element_type=F32)
+        return product[0:8] + product[8:16] + product[16:24]
+
+    def to_groups(value):
+        return times(value, member)
+
+    def to_channels(value):
+        return times(value, member_t)
+
     for copy in st_copies:
         copy.wait_recv()
-    chan = lax.broadcasted_iota(jnp.int32, (C, 128), 0).astype(F32)
-    group = lax.broadcasted_iota(jnp.int32, (C, 128), 1).astype(F32)
-    member = jnp.where(jnp.floor((chan + 0.5) * (1.0 / PER_GROUP)) == group, 1.0, 0.0)
-    chan_t = lax.broadcasted_iota(jnp.int32, (128, C), 1).astype(F32)
-    group_t = lax.broadcasted_iota(jnp.int32, (128, C), 0).astype(F32)
-    member_t = jnp.where(jnp.floor((chan_t + 0.5) * (1.0 / PER_GROUP)) == group_t, 1.0, 0.0)
-
-    def to_groups(value):
-        return jnp.dot(value, member, precision=lax.Precision.HIGHEST, preferred_element_type=F32)
-
-    def to_channels(value):
-        return jnp.dot(value, member_t, precision=lax.Precision.HIGHEST, preferred_element_type=F32)
-
     sums = st[0]
     for i in range(1, STRIPS):
         sums = sums + st[i]
@@ -253,7 +269,7 @@
         )
 
     def turn(s):
-        return jnp.where(s == 0, 1, jnp.where(s == 1, 3, jnp.where(s == 2, 2, 0)))
+        return jnp.where(s == 0, 2, jnp.where(s == 1, 1, jnp.where(s == 2, 3, 0)))
 
     def x_copy(s):
         xq = x_peer(turn(s))
@@ -377,13 +393,11 @@
     sums01 = (zeros8, zeros8)
     sums01 = dactive_step(0, sums01)
     first_bc(0)
-    sums01 = dactive_step(1, sums01)
     first_bc(1)
     first_bc(2)
     first_a()
     first_bc(3)
-    sums01 = dactive_step(2, sums01)
-    sums01 = dactive_step(3, sums01)
+    sums01 = dactive_step(1, sums01)
     sum0 = jnp.sum(sums01[0], axis=0, keepdims=True)
     sum1 = jnp.sum(sums01[1], axis=0, keepdims=True)
     sb[tile, 0:1] = sum1
@@ -392,7 +406,7 @@
     for copy in sb_copies:
         copy.start()
 
-    for i, n in ((0, 1), (1, 3), (2, 2), (3, 0)):
+    for i, n in ((0, 2), (1, 1), (2, 3), (3, 0)):
         xq = x_peer(n)
         for d in (1, 2, 3):
             b2_copy(i, d).wait_recv()
@@ -476,10 +490,6 @@
         return carry
 
     lax.fori_loop(0, ROWS, finish, 0)
-    g2.wait_recv()
-    gc[...] = gz[...] + gzr[...]
-    g3 = remote(gc, gcr, g_send.at[4], g_recv.at[4], on_core)
-    g3.start()
 
     for part in (1, 0, 2):
         assemble(core, part, 0, 0)
@@ -487,13 +497,19 @@
         for part in (1, 0, 2):
             gat_copy(part, dz, dx).wait_recv()
             mate_gat(part, dz, dx).start()
+    for dz, dx in order:
+        for part in (1, 0, 2):
             assemble(core, part, dz, dx)
-    g3.wait_recv()
-    dg_ref[...] = gc[...] + gcr[...]
+    g2.wait_recv()
+    gc[...] = gz[...] + gzr[...]
+    g3 = remote(gc, gcr, g_send.at[4], g_recv.at[4], on_core)
+    g3.start()
     for dz, dx in ((0, 0),) + order:
         for part in (1, 0, 2):
             mate_gat(part, dz, dx).wait_recv()
             assemble(mate, part, dz, dx)
+    g3.wait_recv()
+    dg_ref[...] = gc[...] + gcr[...]
 
     for copy in st_copies + halo + [mate_w] + mate_edge + sb_copies + g1 + [g2, g3]:
         copy.wait_send()
@@ -542,9 +558,12 @@
             buf(5, 9 * CI, 128, dtype=F32),
             buf(2, C, dtype=F32),
         ),
-        in_specs=[anywhere, anywhere, vmem, anywhere, vmem, vmem],
+        in_specs=[anywhere] * 6,
         out_specs=(vmem, vmem, vmem),
         scratch_shapes=[
+            buf(ROWS, W, dtype=jnp.int32),
+            buf(C, dtype=F32),
+            buf(C, dtype=F32),
             buf(ROWS, W, C),
             buf(ROWS, W, C),
             buf(ROWS + 2, W, C),
@@ -584,7 +603,7 @@
             buf(2, C, dtype=F32),
             buf(2, C, dtype=F32),
             buf(2, C, dtype=F32),
-            dma((2,)),
+            dma((5,)),
             dma((9,)),
             dma((7,)),
             dma((7,)),
@@ -623,7 +642,7 @@
             collective_id=0, has_side_effects=True, vmem_limit_bytes=56 * 1024 * 1024
         ),
         cost_estimate=pl.CostEstimate(flops=4 * CELLS * K9 * C, bytes_accessed=13_000_000, transcendentals=CELLS * C),
-    )(features, cotangent, mask[0], conv_weight, gamma, beta)
+    )(features, cotangent, mask, conv_weight, gamma, beta)
     return dfeatures, jnp.concatenate([dweight[j] for j in range(5)], axis=1), dgains
 
 

time: 67.5 us -> 66.2 us (0.981)
  Pallas kernels: 63.6 us -> 62.4 us
    pallas_call x1, Pallas kernels: 63.6 us -> 62.4 us  [shards(): pl.pallas_call(kernel, out_shape=(buf(1, ROWS, W, C), buf(5, 9 * CI, 128,...]
where the time goes in v4:
time: 66.2 us; the launch traced here: 66.1 us
  Pallas kernels  62.4 us (94%)
  local copies, waits for them, and re-layouts  3.01 us (5%)
  between operations  0.68 us (1%)
    pallas_call x1, Pallas kernels, shards(): pl.pallas_call(kernel, out_shape=(buf(1, ROWS, W, C), buf(5, 9 * CI, 128,...  62.4 us
    unnamed x8, local copies, waits for them, and re-layouts  2.98 us

profile of v4, /device:TPU:1, one launch (start us, length us, event | category | flops | bytes accessed | tf_op | source)
XLA Modules:
  0.0 66.1 jit_solution(14506820081496812734)
XLA Ops:
  0.6 62.4 %shard_map.85 = (bf16[1,8,128,640]{3,2,1,0:T(8,128)(2,1)S(1)}, f32[5,720,128]{2,1,0:T(8,128)S(1)}, f32[2,640]{1,0:T(2,128)S(1)}) custom-call(bf16[1,8,128,640]{3,2,1,0:T(8,128)(2,1)} %x_hbm.1, bf16[1,8,128,640]{3,2,1,0:T(8,128)(2,1)} %cot_hbm.1, s32[1,8,128]{2,1,0:T(8,128)} %mask_hbm.1, bf16[3,3,640,640]{3,2,1,0:T(8,128)(2,1)} %w_hbm.1, f32[640]{0:T(1024)} %gamma_hbm.1, ...), custom_call_target="tpu_custom_call" | custom-call | flops 15099494400 | bytes 13000000 | tf_op jit(solution)/shard_map/pallas_call | solution.py:554
  63.0 1.1 %copy.15 = bf16[1,8,128,640]{3,2,1,0:T(8,128)(2,1)} copy(bf16[1,8,128,640]{3,2,1,0:T(8,128)(2,1)S(1)} %get-tuple-element.9) | data formatting | bytes 2621440
  64.1 0.6 copy.16
  64.9 0.0 copy-start
  64.9 1.2 %copy-done = f32[720,640]{1,0:T(8,128)} copy-done((f32[720,640]{1,0:T(8,128)}, f32[720,640]{1,0:T(8,128)S(1)}, u32[]{:S(2)}) %copy-start) | copy-done | bytes 1843224
  (5 shorter events, 0.1 us)
Async XLA Ops:
  64.9 1.2 %copy-start = (f32[720,640]{1,0:T(8,128)}, f32[720,640]{1,0:T(8,128)S(1)}, u32[]{:S(2)}) copy-start(f32[720,640]{1,0:T(8,128)S(1)} %bitcast_dynamic-update-slice_fusion) | copy-start | bytes 5529604

commit v5 on v4

--- a/solution.py
+++ b/solution.py
@@ -555,7 +555,7 @@
         kernel,
         out_shape=(
             buf(1, ROWS, W, C),
-            buf(5, 9 * CI, 128, dtype=F32),
+            buf(5, 9 * CI + 8, 128, dtype=F32),
             buf(2, C, dtype=F32),
         ),
         in_specs=[anywhere] * 6,
@@ -643,7 +643,7 @@
         ),
         cost_estimate=pl.CostEstimate(flops=4 * CELLS * K9 * C, bytes_accessed=13_000_000, transcendentals=CELLS * C),
     )(features, cotangent, mask, conv_weight, gamma, beta)
-    return dfeatures, jnp.concatenate([dweight[j] for j in range(5)], axis=1), dgains
+    return dfeatures, jnp.concatenate([dweight[j, : 9 * CI] for j in range(5)], axis=1), dgains
 
 
 def solution(mesh):

time: 66.2 us -> 66.2 us (level)
  no operation moved by 1% of the time
where the time goes in v5:
time: 66.2 us; the launch traced here: 66.1 us
  Pallas kernels  62.4 us (94%)
  local copies, waits for them, and re-layouts  3.01 us (5%)
  between operations  0.68 us (1%)
    pallas_call x1, Pallas kernels, shards(): pl.pallas_call(kernel, out_shape=(buf(1, ROWS, W, C), buf(5, 9 * CI + 8,...  62.4 us
    unnamed x8, local copies, waits for them, and re-layouts  2.98 us

profile of v5, /device:TPU:1, one launch (start us, length us, event | category | flops | bytes accessed | tf_op | source)
XLA Modules:
  0.0 66.1 jit_solution(17419035603066961319)
XLA Ops:
  0.6 62.4 %shard_map.85 = (bf16[1,8,128,640]{3,2,1,0:T(8,128)(2,1)S(1)}, f32[5,728,128]{2,1,0:T(8,128)S(1)}, f32[2,640]{1,0:T(2,128)S(1)}) custom-call(bf16[1,8,128,640]{3,2,1,0:T(8,128)(2,1)} %x_hbm.1, bf16[1,8,128,640]{3,2,1,0:T(8,128)(2,1)} %cot_hbm.1, s32[1,8,128]{2,1,0:T(8,128)} %mask_hbm.1, bf16[3,3,640,640]{3,2,1,0:T(8,128)(2,1)} %w_hbm.1, f32[640]{0:T(1024)} %gamma_hbm.1, ...), custom_call_target="tpu_custom_call" | custom-call | flops 15099494400 | bytes 13000000 | tf_op jit(solution)/shard_map/pallas_call | solution.py:554
  63.0 1.1 %copy.15 = bf16[1,8,128,640]{3,2,1,0:T(8,128)(2,1)} copy(bf16[1,8,128,640]{3,2,1,0:T(8,128)(2,1)S(1)} %get-tuple-element.9) | data formatting | bytes 2621440
  64.1 0.6 copy.16
  64.9 0.0 copy-start
  64.9 1.2 %copy-done = f32[720,640]{1,0:T(8,128)} copy-done((f32[720,640]{1,0:T(8,128)}, f32[720,640]{1,0:T(8,128)S(1)}, u32[]{:S(2)}) %copy-start) | copy-done | bytes 1843224
  (5 shorter events, 0.1 us)
Async XLA Ops:
  64.9 1.2 %copy-start = (f32[720,640]{1,0:T(8,128)}, f32[720,640]{1,0:T(8,128)S(1)}, u32[]{:S(2)}) copy-start(f32[720,640]{1,0:T(8,128)S(1)} %bitcast_dynamic-update-slice_fusion) | copy-start | bytes 5529604

commit v6 on v5

--- a/solution.py
+++ b/solution.py
@@ -32,7 +32,7 @@
     df, dwv, dg_ref,
     mask_ref, gamma_ref, beta_ref, x, cot, wpad, wpad_m, cols, cols_m, wmat, act_t, act_m, dn,
     part_sum, own1, own2, s1, r1a, r1b, r1c, t2a, t2b, t2c, h2a, h2b, h2c, r2a, r2b, r2c, t3a, t3b, t3c, r3, gat,
-    st, sb, gx, gxr, gz, gzr, gc, gcr,
+    st, sb, gx, gc, gcr,
     load_sem, w_sem,
     st_send, st_recv, sb_send, sb_recv, halo_send, halo_recv,
     wm_send, wm_recv, am_send, am_recv, hm_send, hm_recv,
@@ -74,7 +74,6 @@
     on_y = [place(mx, y_peer(d), mz, core) for d in (1, 2, 3)]
     on_z = [place(mx, my, z_peer(d), core) for d in (1, 2, 3)]
     on_core = place(mx, my, mz, mate)
-    on_zlo = place(mx, my, zhi * 2 + 1 - zlo, core)
 
     def on_tile(d):
         return {"dp": dp, "tile": lax.rem(tile + d, STRIPS)}
@@ -380,6 +379,16 @@
         if i < 3:
             c2_copy(i).start()
 
+    def first_sent(s):
+        mate_act(s * 4).wait_send()
+        mate_act(s * 4 + 1).wait_send()
+        mate_act(s * 4 + 2).wait_send()
+        mate_act(s * 4 + 3).wait_send()
+        x_copy(s).wait_send()
+        for d in (1, 2, 3):
+            y_copy(s, d).wait_send()
+            z_copy(s, d).wait_send()
+
     def first_a():
         for i in range(3):
             x_copy(i).wait_recv()
@@ -394,6 +403,10 @@
     sums01 = dactive_step(0, sums01)
     first_bc(0)
     first_bc(1)
+    for copy in st_copies + halo + [mate_w] + mate_edge:
+        copy.wait_send()
+    for s in range(2):
+        first_sent(s)
     first_bc(2)
     first_a()
     first_bc(3)
@@ -429,17 +442,21 @@
     for d in (1, 3, 2):
         c3_copy(d).start()
 
+    order = ((0, 1), (0, 3), (1, 0), (0, 2), (1, 1), (1, 3), (1, 2))
+
     for copy in sb_copies:
         copy.wait_recv()
     gsum = sb[0]
     for i in range(1, STRIPS):
         gsum = gsum + sb[i]
-    gx[...] = gsum
-    g1 = [remote(gx, gxr.at[d - 1], g_send.at[d - 1], g_recv.at[d - 1], on_x[d - 1]) for d in (1, 2, 3)]
+    gx[zlo, mx] = gsum
+    g1 = []
+    for n, (dz, dx) in enumerate(order):
+        target = place(x_peer(dx), my, zhi * 2 + lax.rem(zlo + dz, 2), core)
+        g1.append(remote(gx.at[zlo, mx], gx.at[zlo, mx], g_send.at[n], g_recv.at[n], target))
     for copy in g1:
         copy.start()
 
-    order = ((0, 1), (0, 3), (1, 0), (0, 2), (1, 1), (1, 3), (1, 2))
 
     def gat_copy(part, dz, dx):
         mine = gat.at[core, zlo, mx, part]
@@ -477,12 +494,6 @@
     second = moments[0:1]
     first = moments[1:2]
 
-    for copy in g1:
-        copy.wait_recv()
-    gz[...] = gx[...] + gxr[0] + gxr[1] + gxr[2]
-    g2 = remote(gz, gzr, g_send.at[3], g_recv.at[3], on_zlo)
-    g2.start()
-
     def finish(i, carry):
         scaled = (x[i].astype(F32) - mean) * inverse
         grad = inverse * (dn[i] * gamma - first - scaled * second) + wpad[i + 1].astype(F32)
@@ -490,6 +501,22 @@
         return carry
 
     lax.fori_loop(0, ROWS, finish, 0)
+    for copy in g1:
+        copy.wait_recv()
+    total = gx[0, 0]
+    for n in range(1, 8):
+        total = total + gx[n // 4, n % 4]
+    gc[...] = total
+    g3 = remote(gc, gcr, g_send.at[7], g_recv.at[7], on_core)
+    g3.start()
+
+    x_copy(2).wait_send()
+    for s in (2, 3):
+        for d in (1, 2, 3):
+            y_copy(s, d).wait_send()
+            z_copy(s, d).wait_send()
+    for copy in sb_copies:
+        copy.wait_send()
 
     for part in (1, 0, 2):
         assemble(core, part, 0, 0)
@@ -500,10 +527,21 @@
     for dz, dx in order:
         for part in (1, 0, 2):
             assemble(core, part, dz, dx)
-    g2.wait_recv()
-    gc[...] = gz[...] + gzr[...]
-    g3 = remote(gc, gcr, g_send.at[4], g_recv.at[4], on_core)
-    g3.start()
+    for i in range(4):
+        for d in (1, 2, 3):
+            a2_copy(i, d).wait_send()
+            b2_copy(i, d).wait_send()
+        if i < 3:
+            c2_copy(i).wait_send()
+    for d in (1, 2, 3):
+        a3_copy(d).wait_send()
+        b3_copy(d).wait_send()
+        c3_copy(d).wait_send()
+    for copy in g1:
+        copy.wait_send()
+    for part in range(3):
+        for dz, dx in order:
+            gat_copy(part, dz, dx).wait_send()
     for dz, dx in ((0, 0),) + order:
         for part in (1, 0, 2):
             mate_gat(part, dz, dx).wait_recv()
@@ -511,35 +549,11 @@
     g3.wait_recv()
     dg_ref[...] = gc[...] + gcr[...]
 
-    for copy in st_copies + halo + [mate_w] + mate_edge + sb_copies + g1 + [g2, g3]:
-        copy.wait_send()
     for part in range(3):
         mate_gat(part, 0, 0).wait_send()
         for dz, dx in order:
-            gat_copy(part, dz, dx).wait_send()
             mate_gat(part, dz, dx).wait_send()
-    for d in (1, 2, 3):
-        a3_copy(d).wait_send()
-        b3_copy(d).wait_send()
-        c3_copy(d).wait_send()
-
-    def drain(s, carry):
-        mate_act(s * 2).wait_send()
-        mate_act(s * 2 + 1).wait_send()
-        for d in (1, 2, 3):
-            y_copy(s, d).wait_send()
-            z_copy(s, d).wait_send()
-            a2_copy(s, d).wait_send()
-            b2_copy(s, d).wait_send()
-
-        @pl.when(s < 3)
-        def _():
-            x_copy(s).wait_send()
-            c2_copy(s).wait_send()
-
-        return carry
-
-    lax.fori_loop(0, 4, drain, 0)
+    g3.wait_send()
 
 
 def shards(features, cotangent, mask, conv_weight, gamma, beta):
@@ -597,10 +611,7 @@
             buf(2, 2, 4, 3, *panel),
             buf(STRIPS, 2, C, dtype=F32),
             buf(STRIPS, 2, C, dtype=F32),
-            buf(2, C, dtype=F32),
-            buf(3, 2, C, dtype=F32),
-            buf(2, C, dtype=F32),
-            buf(2, C, dtype=F32),
+            buf(2, 4, 2, C, dtype=F32),
             buf(2, C, dtype=F32),
             buf(2, C, dtype=F32),
             dma((5,)),
@@ -635,8 +646,8 @@
             dma((3, 8)),
             dma((3, 8)),
             dma((3, 8)),
-            dma((5,)),
-            dma((5,)),
+            dma((8,)),
+            dma((8,)),
         ],
         compiler_params=pltpu.CompilerParams(
             collective_id=0, has_side_effects=True, vmem_limit_bytes=56 * 1024 * 1024

time: 66.2 us -> 66.2 us (level)
  no operation moved by 1% of the time
where the time goes in v6:
time: 66.2 us; the launch traced here: 66.1 us
  Pallas kernels  62.4 us (94%)
  local copies, waits for them, and re-layouts  3.01 us (5%)
  between operations  0.68 us (1%)
    pallas_call x1, Pallas kernels, shards(): pl.pallas_call(kernel, out_shape=(buf(1, ROWS, W, C), buf(5, 9 * CI + 8,...  62.4 us
    unnamed x8, local copies, waits for them, and re-layouts  2.98 us

profile of v6, /device:TPU:1, one launch (start us, length us, event | category | flops | bytes accessed | tf_op | source)
XLA Modules:
  0.0 66.1 jit_solution(10468677187448338385)
XLA Ops:
  0.6 62.4 %shard_map.85 = (bf16[1,8,128,640]{3,2,1,0:T(8,128)(2,1)S(1)}, f32[5,728,128]{2,1,0:T(8,128)S(1)}, f32[2,640]{1,0:T(2,128)S(1)}) custom-call(bf16[1,8,128,640]{3,2,1,0:T(8,128)(2,1)} %x_hbm.1, bf16[1,8,128,640]{3,2,1,0:T(8,128)(2,1)} %cot_hbm.1, s32[1,8,128]{2,1,0:T(8,128)} %mask_hbm.1, bf16[3,3,640,640]{3,2,1,0:T(8,128)(2,1)} %w_hbm.1, f32[640]{0:T(1024)} %gamma_hbm.1, ...), custom_call_target="tpu_custom_call" | custom-call | flops 15099494400 | bytes 13000000 | tf_op jit(solution)/shard_map/pallas_call | solution.py:568
  63.0 1.1 %copy.15 = bf16[1,8,128,640]{3,2,1,0:T(8,128)(2,1)} copy(bf16[1,8,128,640]{3,2,1,0:T(8,128)(2,1)S(1)} %get-tuple-element.9) | data formatting | bytes 2621440
  64.1 0.6 copy.16
  64.9 0.0 copy-start
  64.9 1.2 %copy-done = f32[720,640]{1,0:T(8,128)} copy-done((f32[720,640]{1,0:T(8,128)}, f32[720,640]{1,0:T(8,128)S(1)}, u32[]{:S(2)}) %copy-start) | copy-done | bytes 1843224
  (5 shorter events, 0.1 us)
Async XLA Ops:
  64.9 1.2 %copy-start = (f32[720,640]{1,0:T(8,128)}, f32[720,640]{1,0:T(8,128)S(1)}, u32[]{:S(2)}) copy-start(f32[720,640]{1,0:T(8,128)S(1)} %bitcast_dynamic-update-slice_fusion) | copy-start | bytes 5529604

commit v7 on v6

--- a/solution.py
+++ b/solution.py
@@ -407,8 +407,8 @@
         copy.wait_send()
     for s in range(2):
         first_sent(s)
+    first_a()
     first_bc(2)
-    first_a()
     first_bc(3)
     sums01 = dactive_step(1, sums01)
     sum0 = jnp.sum(sums01[0], axis=0, keepdims=True)

time: 66.2 us -> 66.2 us (level)
  no operation moved by 1% of the time
where the time goes in v7:
time: 66.2 us; the launch traced here: 66.1 us
  Pallas kernels  62.4 us (94%)
  local copies, waits for them, and re-layouts  3.01 us (5%)
  between operations  0.68 us (1%)
    pallas_call x1, Pallas kernels, shards(): pl.pallas_call(kernel, out_shape=(buf(1, ROWS, W, C), buf(5, 9 * CI + 8,...  62.4 us
    unnamed x8, local copies, waits for them, and re-layouts  2.98 us

profile of v7, /device:TPU:1, one launch (start us, length us, event | category | flops | bytes accessed | tf_op | source)
XLA Modules:
  0.0 66.1 jit_solution(13893518850666051266)
XLA Ops:
  0.6 62.4 %shard_map.85 = (bf16[1,8,128,640]{3,2,1,0:T(8,128)(2,1)S(1)}, f32[5,728,128]{2,1,0:T(8,128)S(1)}, f32[2,640]{1,0:T(2,128)S(1)}) custom-call(bf16[1,8,128,640]{3,2,1,0:T(8,128)(2,1)} %x_hbm.1, bf16[1,8,128,640]{3,2,1,0:T(8,128)(2,1)} %cot_hbm.1, s32[1,8,128]{2,1,0:T(8,128)} %mask_hbm.1, bf16[3,3,640,640]{3,2,1,0:T(8,128)(2,1)} %w_hbm.1, f32[640]{0:T(1024)} %gamma_hbm.1, ...), custom_call_target="tpu_custom_call" | custom-call | flops 15099494400 | bytes 13000000 | tf_op jit(solution)/shard_map/pallas_call | solution.py:568
  63.0 1.1 %copy.15 = bf16[1,8,128,640]{3,2,1,0:T(8,128)(2,1)} copy(bf16[1,8,128,640]{3,2,1,0:T(8,128)(2,1)S(1)} %get-tuple-element.9) | data formatting | bytes 2621440
  64.1 0.6 copy.16
  64.9 0.0 copy-start
  64.9 1.2 %copy-done = f32[720,640]{1,0:T(8,128)} copy-done((f32[720,640]{1,0:T(8,128)}, f32[720,640]{1,0:T(8,128)S(1)}, u32[]{:S(2)}) %copy-start) | copy-done | bytes 1843224
  (5 shorter events, 0.1 us)
Async XLA Ops:
  64.9 1.2 %copy-start = (f32[720,640]{1,0:T(8,128)}, f32[720,640]{1,0:T(8,128)S(1)}, u32[]{:S(2)}) copy-start(f32[720,640]{1,0:T(8,128)S(1)} %bitcast_dynamic-update-slice_fusion) | copy-start | bytes 5529604
